TPU v7x, 512 devices: a whole 4x4x16 slice. The times are simulated.
512 devices in a mesh: img: 8 (over x, core), cls: 8 (over z_lo), tpl: 8 (over z_hi, y).
Axes of the slice: x: 4, y: 4, z: 16 (z_hi: 2, z_lo: 8; z = z_hi * 8 + z_lo), core: 2. Of those that a mesh axis runs over, the one named last changes fastest.
Arguments:
- images: bfloat16 [16384, 1280], P(('img', 'tpl')), may hold values from -5 to 5
- labels: int32 [16384], P(('img', 'tpl')), may hold values from 0 to 4095
- templates: bfloat16 [32, 4096, 1280], P('tpl', ('cls', 'img')), may hold values from -0.125 to 0.125
- projection: bfloat16 [1280, 1280], P('img', 'cls'), may hold values from -0.08441157 to 0.08441157
Outputs:
- grad_templates: bfloat16 [32, 4096, 1280], P('tpl', ('cls', 'img'))
- grad_projection: float32 [1280, 1280], P('img', 'cls')
All inputs are finite; a program needn't handle non-finite values.
Results may differ from a plain program's by a relative error of at most 0.011.
Values may be sent and summed in bfloat16 or wider, within the bound.
A program may use at most 64 MiB of HBM per device.

v0:
```python
import jax
import jax.numpy as jnp
from jax import lax
from jax.sharding import PartitionSpec as P

logit_scale = 50.0
epsilon = 1e-06


def inverse_norm(values):
    return lax.rsqrt(jnp.sum(values * values, axis=-1, keepdims=True) + epsilon)


def body(images, labels, templates, projection):
    tpl_count = templates.shape[0]
    cls_count = templates.shape[1]
    feat_width = templates.shape[2]
    tpl_total = tpl_count * lax.axis_size("tpl")
    img_count = lax.axis_size("img")
    wide_proj = lax.all_gather(projection, "cls", axis=1, tiled=True)
    full_proj = lax.all_gather(wide_proj, "img", axis=0, tiled=True)
    flat_tpl = templates.reshape(tpl_count * cls_count, feat_width)
    text_z = jnp.dot(flat_tpl, full_proj, preferred_element_type=jnp.float32)
    text_rz = inverse_norm(text_z)
    text_u = text_z * text_rz
    u_three = text_u.reshape(tpl_count, cls_count, feat_width)
    local_sum = jnp.sum(u_three, axis=0)
    mean_emb = lax.psum(local_sum, "tpl") / tpl_total
    mean_rn = inverse_norm(mean_emb)
    class_w = mean_emb * mean_rn
    class_b = class_w.astype(jnp.bfloat16)
    img_f = images.astype(jnp.float32)
    img_b = (img_f * inverse_norm(img_f)).astype(jnp.bfloat16)
    all_img, all_labels = (
        lax.all_gather(img_b, "img", axis=0, tiled=True),
        lax.all_gather(labels, "img", axis=0, tiled=True),
    )
    scores = logit_scale * jnp.einsum(
        "cd,nd->cn", class_b, all_img, preferred_element_type=jnp.float32
    )
    exp_scores = jnp.exp(scores)
    totals = lax.psum(jnp.sum(exp_scores, axis=0), ("img", "cls"))
    first_id = (lax.axis_index("cls") * img_count + lax.axis_index("img")) * cls_count
    class_ids = first_id + lax.broadcasted_iota(jnp.int32, (cls_count, 1), 0)
    one_hot = (all_labels[None, :] == class_ids).astype(jnp.float32)
    grad_logit = (exp_scores / totals[None, :] - one_hot).astype(jnp.bfloat16)
    partial_value = logit_scale * jnp.dot(grad_logit, all_img, preferred_element_type=jnp.float32)
    class_g = lax.psum(partial_value, "tpl")
    dot_wg = jnp.sum(class_w * class_g, axis=1, keepdims=True)
    grad_mean = (class_g - class_w * dot_wg) * mean_rn
    per_u = grad_mean / tpl_total
    inner_prod = jnp.sum(u_three * per_u[None], axis=2, keepdims=True)
    grad_z = (
        (per_u[None] - u_three * inner_prod) * text_rz.reshape(tpl_count, cls_count, 1)
    ).astype(jnp.bfloat16)
    grad_flat = grad_z.reshape(tpl_count * cls_count, feat_width)
    grad_tpl = lax.dot_general(
        grad_flat, full_proj, (((1,), (1,)), ((), ())), preferred_element_type=jnp.float32
    )
    grad_templates = grad_tpl.astype(jnp.bfloat16).reshape(tpl_count, cls_count, feat_width)
    tpl_columns = lax.all_to_all(flat_tpl, "img", split_axis=1, concat_axis=0, tiled=True)
    partial_proj = lax.dot_general(
        tpl_columns,
        lax.all_gather(grad_flat, "img", axis=0, tiled=True),
        (((0,), (0,)), ((), ())),
        preferred_element_type=jnp.float32,
    )
    shared_proj = lax.psum_scatter(
        partial_proj.astype(jnp.bfloat16), "cls", scatter_dimension=1, tiled=True
    )
    grad_projection = lax.psum(shared_proj, "tpl").astype(jnp.float32)
    return (grad_templates, grad_projection)


def solution(mesh):
    in_specs = (
        P(("img", "tpl"), None),
        P(("img", "tpl")),
        P("tpl", ("cls", "img"), None),
        P("img", "cls"),
    )
    out_specs = (P("tpl", ("cls", "img"), None), P("img", "cls"))
    return jax.shard_map(body, mesh=mesh, in_specs=in_specs, out_specs=out_specs, check_vma=False)
```

profile of v0, /device:TPU:1, one launch (start us, length us, event | category | flops | bytes accessed | tf_op | source)
XLA Modules:
  0.0 846.6 jit_solution(12290353934308617125)
XLA Ops:
  7.2 1.0 copy.10
  8.3 47.0 %all_gather.15 = bf16[160,1280]{0,1:T(8,128)(2,1)S(1)} all-gather(bf16[160,160]{0,1:T(8,128)(2,1)S(1)} %copy.10), channel_id=1, replica_groups=mesh['img'=8,'cls'=8,'tpl'=8] {'cls'}, dimensions={1}, use_global_device_ids=true | all-gather | bytes 460800 | tf_op jit(solution)/shard_map/all_gather | solution.py:20
  56.5 43.4 %all-gather.5.cloned.1.call-done = bf16[1280,1280]{1,0:T(8,128)(2,1)} async-done(((bf16[160,1280]{1,0:T(8,128)(2,1)}), bf16[1280,1280]{1,0:T(8,128)(2,1)}) %all-gather.5.cloned.1.call-update) | async-done | bytes 3276816 | tf_op jit(solution)/shard_map/all_gather | solution.py:21
  99.9 3.0 multiply_reduce_fusion
  104.0 1.0 fusion.3
  105.1 9.3 %all-gather = s32[8,1,256]{2,1,0:T(1,128)S(1)} all-gather(s32[1,1,256]{2,1,0:T(1,128)S(1)} %bitcast.36), channel_id=1, replica_groups=mesh['img'=8,'cls'=8,'tpl'=8] {'img'}, dimensions={0}, use_global_device_ids=true | all-gather | bytes 9216 | tf_op jit(solution)/shard_map/all_gather | solution.py:36
  114.5 136.2 %all-reduce.3.cloned.1.call-done = f32[64,1280]{1,0:T(8,128)} async-done(((f32[64,1280]{1,0:T(8,128)}), f32[64,1280]{1,0:T(8,128)}) %all-reduce.3.cloned.1.call-update) | async-done | bytes 327696 | tf_op jit(solution)/shard_map/psum | solution.py:28
  250.6 1.1 multiply_reduce_fusion.2
  251.8 42.0 %all-gather.7.cloned.1.call-done = bf16[2048,1280]{1,0:T(8,128)(2,1)} async-done(((bf16[256,1280]{1,0:T(8,128)(2,1)}), bf16[2048,1280]{1,0:T(8,128)(2,1)}) %all-gather.7.cloned.1.call-update) | async-done | bytes 5242896 | tf_op jit(solution)/shard_map/all_gather | solution.py:35
  293.7 4.3 fusion.11
  298.1 194.9 %psum.29 = f32[2048]{0:T(1024)S(1)} all-reduce(f32[2048]{0:T(1024)S(1)} %get-tuple-element.6), channel_id=1, replica_groups=mesh['img'=8,'cls'=8,'tpl'=8] {'img','cls'}, use_global_device_ids=true, to_apply=%region_6.0 | all-reduce | flops 2048 | bytes 16384 | tf_op jit(solution)/shard_map/psum | solution.py:42
  493.0 4.3 convolution_multiply_fusion
  497.4 166.2 %all-reduce.5.cloned.1.call-done = f32[64,1280]{1,0:T(8,128)} async-done(((f32[64,1280]{1,0:T(8,128)}), f32[64,1280]{1,0:T(8,128)}) %all-reduce.5.cloned.1.call-update) | async-done | bytes 327696 | tf_op jit(solution)/shard_map/psum | solution.py:48
  663.6 1.2 multiply_reduce_fusion.1
  664.8 1.1 multiply_multiply_fusion
  666.2 1.1 fusion.6
  667.4 1.3 all_to_all.14
  669.7 27.5 %all_to_all.19 = bf16[256,8,160]{0,2,1:T(8,128)(2,1)S(1)} all-to-all(bf16[256,8,160]{0,2,1:T(8,128)(2,1)S(1)} %copy.12), channel_id=1, replica_groups=mesh['img'=8,'cls'=8,'tpl'=8] {'img'}, dimensions={1} | all-to-all | bytes 1310720 | tf_op jit(solution)/shard_map/all_to_all | solution.py:61
  697.2 16.6 %all-gather.9.cloned.1.call-done = bf16[2048,1280]{1,0:T(8,128)(2,1)} async-done(((bf16[256,1280]{1,0:T(8,128)(2,1)}), bf16[2048,1280]{1,0:T(8,128)(2,1)}) %all-gather.9.cloned.1.call-update) | async-done | bytes 5242896 | tf_op jit(solution)/shard_map/all_gather | solution.py:64
  713.8 3.5 fusion
  717.3 1.1 copy.14
  718.5 3.8 convolution_convert_fusion
  722.3 49.5 %reduce-scatter.4.cloned.1.call-done = bf16[160,160]{1,0:T(8,128)(2,1)} async-done(((bf16[1280,160]{1,0:T(8,128)(2,1)}), bf16[160,160]{1,0:T(8,128)(2,1)}) %reduce-scatter.4.cloned.1.call-update) | async-done | bytes 51216
  772.8 66.3 %psum.31 = bf16[160,160]{1,0:T(8,128)(2,1)S(1)} all-reduce(bf16[160,160]{1,0:T(8,128)(2,1)S(1)} %copy.15), channel_id=1, replica_groups=mesh['img'=8,'cls'=8,'tpl'=8] {'tpl'}, use_global_device_ids=true, to_apply=%region_11.0 | all-reduce | flops 25600 | bytes 102400 | tf_op jit(solution)/shard_map/psum | solution.py:71
  (37 shorter events, 5.6 us)
Async XLA Ops:
  7.2 49.1 %copy-start.1 = (bf16[256,1280]{1,0:T(8,128)(2,1)S(1)}, bf16[256,1280]{1,0:T(8,128)(2,1)}, u32[]{:S(2)}) copy-start(bf16[256,1280]{1,0:T(8,128)(2,1)} %param.4) | copy-start | bytes 1966084
  7.2 92.7 %all-gather.5.cloned.1.call-start = ((), (), s32[]{:S(2)}) async-start(), calls=%async_computation.2 | async-start | bytes 3686400 | tf_op jit(solution)/shard_map/all_gather | solution.py:21
  8.3 91.6 %copy-start.3 = (bf16[4,64,1280]{2,1,0:T(8,128)(2,1)S(1)}, bf16[4,64,1280]{2,1,0:T(8,128)(2,1)}, u32[]{:S(2)}) copy-start(bf16[4,64,1280]{2,1,0:T(8,128)(2,1)} %param.6) | copy-start | bytes 1966084
  56.3 194.4 %all-reduce.3.cloned.1.call-start = ((), (), s32[]{:S(2)}) async-start(), calls=%async_computation.3 | async-start | bytes 655360 | tf_op jit(solution)/shard_map/psum | solution.py:28
  104.0 1.2 copy-start.5
  104.0 189.7 %all-gather.7.cloned.1.call-start = ((), (), s32[]{:S(2)}) async-start(), calls=%async_computation.4 | async-start | bytes 5898240 | tf_op jit(solution)/shard_map/all_gather | solution.py:35
  105.1 558.5 %all-reduce.5.cloned.1.call-start = ((), (), s32[]{:S(2)}) async-start(), calls=%async_computation.5 | async-start | bytes 655360 | tf_op jit(solution)/shard_map/psum | solution.py:48
  493.0 170.6 %copy-start = (f32[64,1280]{1,0:T(8,128)S(1)}, f32[64,1280]{1,0:T(8,128)}, u32[]{:S(2)}) copy-start(f32[64,1280]{1,0:T(8,128)} %all-reduce.3.cloned.1.call-done) | copy-start | bytes 983044
  497.4 216.5 %all-gather.9.cloned.1.call-start = ((), (), s32[]{:S(2)}) async-start(), calls=%async_computation.6 | async-start | bytes 5898240 | tf_op jit(solution)/shard_map/all_gather | solution.py:64
  666.2 1.2 copy-start.4
  667.3 104.5 %reduce-scatter.4.cloned.1.call-start = ((), (), s32[]{:S(2)}) async-start(), calls=%async_computation.7 | async-start | bytes 737280
  717.3 1.1 copy-start.2
Sparse Core Ops, SparseCore 0:
  56.4 43.4 all-gather.4
  104.1 146.4 all-reduce.2
  253.6 40.1 all-gather.6
  497.5 166.0 all-reduce.4
  667.4 46.3 all-gather.8
  718.6 53.1 reduce-scatter.3
where the time goes:
time: 857 us; the launch traced here: 847 us
  waiting for transfers between devices  454 us (53%)
  blocking collectives  345 us (40%)
  matrix products  19 us (2%)
  between operations  14.3 us (2%)
    psum x1, blocking collectives, body(): totals = lax.psum(jnp.sum(exp_scores, axis=0), ('img', 'cls'))  195 us
    psum x1, waiting for transfers between devices, body(): class_g = lax.psum(partial_value, 'tpl')  166 us
    psum x1, waiting for transfers between devices, body(): mean_emb = lax.psum(local_sum, 'tpl') / tpl_total  136 us
    psum x1, blocking collectives, body(): grad_projection = lax.psum(shared_proj, 'tpl').astype(jnp.float32)  66.3 us
    unnamed x7, waiting for transfers between devices  49.6 us
    all_gather x1, blocking collectives, body(): wide_proj = lax.all_gather(projection, 'cls', axis=1, tiled=True)  47 us
    all_gather x1, waiting for transfers between devices, body(): full_proj = lax.all_gather(wide_proj, 'img', axis=0, tiled=True)  43.4 us
    all_gather x1, waiting for transfers between devices, body(): lax.all_gather(img_b, 'img', axis=0, tiled=True)  42 us
  transfers between devices with their start and end apart: 6, of which 6 were waited for; matrix products, arithmetic and copies ran while one was open for 1% of the time, Pallas kernels for 0%

commit v1 on v0

v1 whole, which is shorter than its diff:
```python
import jax
import jax.numpy as jnp
from jax import lax
from jax.experimental import pallas as pl
from jax.experimental.pallas import tpu as pltpu
from jax.sharding import PartitionSpec as P

SCALE = 50.0
EPS = 1e-06
TPL = 32
MESH = pl.DeviceIdType.MESH
BF = jnp.bfloat16
F32 = jnp.float32
PLANE = [(a, b) for a in range(4) for b in range(4) if (a, b) != (0, 0)]
RING = (4, -4, 3, -3, 2, -2, 1, -1)


def inv_norm(v):
    return lax.rsqrt(jnp.sum(v * v, axis=-1, keepdims=True) + EPS)


def device(x, k, y, zh, zl):
    return (x * 2 + k, zl, zh * 4 + y)


class Copies:
    def __init__(self, send, recv):
        self.send, self.recv, self.used = send, recv, 0
        self.open = []

    def __call__(self, src, dst, to):
        n = self.used
        self.used += 1
        cp = pltpu.make_async_remote_copy(
            src_ref=src, dst_ref=dst, send_sem=self.send.at[n], recv_sem=self.recv.at[n],
            device_id=to, device_id_type=MESH)
        cp.start()
        self.open.append(cp)
        return cp

    def finish(self):
        for cp in self.open:
            cp.wait_send()


N_COPIES = 120


def kernel(images, labels, tpl, tplt, proj, gt_out, gp_out,
           wf, pk, pf, zbuf, rzbuf, s_send, s_recv, c_send, c_recv, mbuf, cb, img, lab,
           ebuf, e_send, e_one, e_two, e_recv, gbuf, cg_send, cg_recv, f_send, f_recv, gs, gz, tx,
           hs, hr, rs, w_recv, h_send, h_recv, hy, send_sem, recv_sem):
    i = lax.axis_index("img")
    c = lax.axis_index("cls")
    t = lax.axis_index("tpl")
    x, k, y, zh = i // 2, i % 2, t % 4, t // 4
    z = zh * 8 + c
    other = 1 - k

    def at_plane(dx, dy):
        return (x + dx) % 4, (y + dy) % 4

    def to_plane(dx, dy):
        px, py = at_plane(dx, dy)
        return device(px, k, py, zh, c)

    def to_ring(d):
        n = (z + d + 16) % 16
        return device(x, k, y, n // 8, n % 8)

    sibling = device(x, other, y, zh, c)
    across = device(x, k, y, 1 - zh, c)

    barrier = pltpu.get_barrier_semaphore()
    for dx, dy in PLANE:
        pl.semaphore_signal(barrier, inc=1, device_id=to_plane(dx, dy), device_id_type=MESH)
    for d in range(1, 16):
        pl.semaphore_signal(barrier, inc=1, device_id=to_ring(d), device_id_type=MESH)
    pl.semaphore_signal(barrier, inc=1, device_id=sibling, device_id_type=MESH)

    copy = Copies(send_sem, recv_sem)

    wf[...] = jnp.zeros_like(wf)
    wf[:, 0:160] = proj[...].astype(F32)
    pk[c] = pltpu.roll(wf[...], 32 * (c % 4), 1).astype(BF)

    pl.semaphore_wait(barrier, 31)

    cols = []
    for d in RING:
        if d == 4:
            part = pk.at[c, pl.ds(0, 80)]
        elif d == -4:
            part = pk.at[c, pl.ds(80, 80)]
        else:
            part = pk.at[c]
        cols.append(copy(part, part, to_ring(d)))

    img_f = images[...].astype(F32)
    img[k] = (img_f * inv_norm(img_f)).astype(BF)
    lab[k] = labels[...]
    to_img = copy(img.at[k], img.at[k], sibling)
    to_lab = copy(lab.at[k], lab.at[k], sibling)
    to_tx = copy(tplt.at[other], tx, sibling)

    for cp in cols:
        cp.wait_recv()
    for h in range(2):
        b = h * 4
        tiles = [
            pk[b, :, 0:128],
            pk[b, :, 128:256] + pk[b + 1, :, 0:128],
            pk[b + 1, :, 128:256] + pk[b + 2, :, 0:128],
            pk[b + 2, :, 128:256] + pk[b + 3, :, 0:128],
            pk[b + 3, :, 128:256],
        ]
        for j, tile in enumerate(tiles):
            o = (h * 5 + j) * 128
            pf[i, :, o:o + 128] = tile

    rows = [copy(pf.at[i], pf.at[i], device((x + dx) % 4, k, y, zh, c)) for dx in (1, 3, 2)]
    shared = [copy(pf.at[i], pf.at[i], sibling)]
    for dx, cp in zip((1, 3, 2), rows):
        cp.wait_recv()
        src = ((x - dx + 4) % 4) * 2 + k
        shared.append(copy(pf.at[src], pf.at[src], sibling))
    for cp in shared:
        cp.wait_recv()

    def project(n, _):
        o = pl.ds(pl.multiple_of(n * 256, 256), 256)
        zbuf[:, o] = jnp.dot(tpl[...], pf[:, :, o].reshape(1280, 256), preferred_element_type=F32)
        return 0
    lax.fori_loop(0, 5, project, 0)
    rz = inv_norm(zbuf[...])
    rzbuf[...] = rz
    zbuf[...] = zbuf[...] * rz
    total = zbuf[0:64] + zbuf[64:128] + zbuf[128:192] + zbuf[192:256]
    s_send[...] = total.astype(BF).reshape(4, 16, 1280)

    got = [copy(s_send.at[(y + d) % 4], s_recv.at[d - 1], to_plane(0, d)) for d in (2, 1, 3)]
    for cp in got:
        cp.wait_recv()
    own = s_send[y].astype(F32)
    for d in range(3):
        own = own + s_recv[d].astype(F32)
    c_send[...] = own.astype(BF)
    copy(c_send, c_recv, across).wait_recv()
    mbuf[x, y] = ((c_send[...].astype(F32) + c_recv[...].astype(F32)) / TPL).astype(BF)

    got = [copy(mbuf.at[x, y], mbuf.at[x, y], to_plane(dx, dy)) for dx, dy in PLANE]
    to_img.wait_recv()
    to_lab.wait_recv()
    to_tx.wait_recv()
    for cp in got:
        cp.wait_recv()

    mean = mbuf[...].reshape(256, 1280).astype(F32)
    cb[...] = (mean * inv_norm(mean)).astype(BF)
    for s in range(2):
        sc = lax.dot_general(cb[...], img[s], (((1,), (1,)), ((), ())), preferred_element_type=F32)
        ebuf[:, s * 256:(s + 1) * 256] = jnp.exp(SCALE * sc)
    e_send[...] = jnp.sum(ebuf[...].reshape(32, 8, 512), axis=0)
    copy(e_send, e_one, sibling).wait_recv()
    e_two[...] = e_send[...] + e_one[...]
    got = [copy(e_two, e_recv.at[d - 1], device(x, k, y, zh, (c + d) % 8)) for d in range(1, 8)]
    row = lax.broadcasted_iota(jnp.int32, (256, 1), 0)
    ids = (c * 8 + (row // 64) * 2 + k) * 64 + row % 64
    for cp in got:
        cp.wait_recv()
    tot = e_two[...]
    for d in range(7):
        tot = tot + e_recv[d]
    inv = 1.0 / jnp.sum(tot, axis=0, keepdims=True)
    for s in range(2):
        part = slice(s * 256, (s + 1) * 256)
        hot = (lab[s, 0:1, :] == ids).astype(F32)
        gbuf[:, part] = (ebuf[:, part] * inv[:, part] - hot).astype(BF)

    def class_grad(n, _):
        o = pl.ds(pl.multiple_of(n * 256, 256), 256)
        v = jnp.dot(gbuf[...], img[:, :, o].reshape(512, 256), preferred_element_type=F32)
        cg_send[:, :, :, o] = (SCALE * v).astype(BF).reshape(4, 4, 16, 256)
        return 0
    lax.fori_loop(0, 5, class_grad, 0)

    got = []
    for n, (dx, dy) in enumerate(PLANE):
        px, py = at_plane(dx, dy)
        got.append(copy(cg_send.at[px, py], cg_recv.at[n], to_plane(dx, dy)))
    for cp in got:
        cp.wait_recv()
    own = cg_send[x, y].astype(F32)
    for n in range(15):
        own = own + cg_recv[n].astype(F32)
    f_send[...] = own.astype(BF)
    copy(f_send, f_recv, across).wait_recv()
    gs[y] = (f_send[...].astype(F32) + f_recv[...].astype(F32)).astype(BF)
    got = [copy(gs.at[y], gs.at[y], to_plane(0, d)) for d in (2, 1, 3)]
    mean = mbuf[x].reshape(64, 1280).astype(F32)
    rn = inv_norm(mean)
    class_w = mean * rn
    for cp in got:
        cp.wait_recv()

    class_g = gs[...].reshape(64, 1280).astype(F32)
    dot_wg = jnp.sum(class_w * class_g, axis=1, keepdims=True)
    per_u = (class_g - class_w * dot_wg) * rn / TPL
    for n in range(4):
        rows_n = slice(n * 64, (n + 1) * 64)
        u = zbuf[rows_n]
        inner = jnp.sum(u * per_u, axis=1, keepdims=True)
        gz[k, rows_n] = ((per_u - u * inner) * rzbuf[rows_n]).astype(BF)

    copy(gz.at[k], gz.at[k], sibling).wait_recv()

    got = []
    for dx in (2, 1, 3, 0):
        px = (x + dx) % 4

        def product(n, _):
            o = pl.ds(pl.multiple_of(n * 256, 256), 256)
            v = jnp.dot(tplt[k, px], gz[k, :, o], preferred_element_type=F32)
            v = v + jnp.dot(tx[px], gz[other, :, o], preferred_element_type=F32)
            hs[px, :, o] = v.astype(BF)
            return 0
        lax.fori_loop(0, 5, product, 0)
        for dy in (2, 1, 3, 0):
            if (dx, dy) == (0, 0):
                continue
            py = (y + dy) % 4
            start = pl.multiple_of(jnp.minimum(48 * py, 112), 16)
            got.append(copy(hs.at[px, pl.ds(start, 48)], hr.at[PLANE.index((dx, dy))], to_plane(dx, dy)))

    for m in range(4):
        w = pf[2 * m:2 * m + 2].reshape(320, 1280)
        v = lax.dot_general(gz[k], w, (((1,), (1,)), ((), ())), preferred_element_type=F32)
        gt_out[:, m * 320:(m + 1) * 320] = v.astype(BF)

    for cp in got:
        cp.wait_recv()
    own = hs[x, pl.ds(pl.multiple_of(jnp.minimum(48 * y, 112), 16), 48)].astype(F32)
    for n in range(15):
        own = own + hr[n].astype(F32)
    rs[...] = own.astype(BF)

    def window(cc):
        return pl.ds(pl.multiple_of(128 * ((5 * cc) // 4), 128), 256)

    got = []
    for n, d in enumerate((4, 3, -3, 2, -2, 1, -1)):
        got.append(copy(rs.at[:, window((c + d + 8) % 8)], w_recv.at[n], to_ring(d)))
    for cp in got:
        cp.wait_recv()
    own = rs[:, window(c)].astype(F32)
    for n in range(7):
        own = own + w_recv[n].astype(F32)
    h_send[...] = own.astype(BF)
    copy(h_send, h_recv, across).wait_recv()
    hy[y] = (h_send[...].astype(F32) + h_recv[...].astype(F32)).astype(BF)
    got = [copy(hy.at[y], hy.at[y], to_plane(0, d)) for d in (2, 1, 3)]
    for cp in got:
        cp.wait_recv()
    for n in range(4):
        v = pltpu.roll(hy[n].astype(F32), (256 - 32 * (c % 4)) % 256, 1)[:, 0:160]
        if n < 3:
            gp_out[48 * n:48 * n + 48] = v
        else:
            gp_out[144:160] = v[32:48]
    copy.finish()


def body(images, labels, templates, projection):
    flat = templates.reshape(256, 1280)
    tplt = flat.T.reshape(4, 2, 160, 256).transpose(1, 0, 2, 3)
    lab = jnp.broadcast_to(labels.reshape(1, 256), (8, 256))
    vm = pl.BlockSpec(memory_space=pltpu.VMEM)
    scratch = [
        ((160, 256), F32), ((8, 160, 256), BF), ((8, 160, 1280), BF), ((256, 1280), F32), ((256, 1), F32),
        ((4, 16, 1280), BF), ((3, 16, 1280), BF), ((16, 1280), BF), ((16, 1280), BF),
        ((4, 4, 16, 1280), BF), ((256, 1280), BF), ((2, 256, 1280), BF), ((2, 8, 256), jnp.int32),
        ((256, 512), F32), ((8, 512), F32), ((8, 512), F32), ((8, 512), F32), ((7, 8, 512), F32),
        ((256, 512), BF), ((4, 4, 16, 1280), BF), ((15, 16, 1280), BF), ((16, 1280), BF), ((16, 1280), BF),
        ((4, 16, 1280), BF), ((2, 256, 1280), BF), ((4, 160, 256), BF),
        ((4, 160, 1280), BF), ((15, 48, 1280), BF), ((48, 1280), BF), ((7, 48, 256), BF),
        ((48, 256), BF), ((48, 256), BF), ((4, 48, 256), BF),
    ]
    gt, gp = pl.pallas_call(
        kernel,
        out_shape=(jax.ShapeDtypeStruct((256, 1280), BF), jax.ShapeDtypeStruct((160, 160), F32)),
        in_specs=[vm] * 5,
        out_specs=(vm, vm),
        scratch_shapes=[pltpu.VMEM(s, d) for s, d in scratch]
        + [pltpu.SemaphoreType.DMA((N_COPIES,)), pltpu.SemaphoreType.DMA((N_COPIES,))],
        compiler_params=pltpu.CompilerParams(
            collective_id=0, has_side_effects=True, vmem_limit_bytes=50 << 20),
    )(images, lab, flat, tplt, projection)
    return gt.reshape(templates.shape), gp


def solution(mesh):
    in_specs = (
        P(("img", "tpl"), None),
        P(("img", "tpl")),
        P("tpl", ("cls", "img"), None),
        P("img", "cls"),
    )
    out_specs = (P("tpl", ("cls", "img"), None), P("img", "cls"))
    return jax.shard_map(body, mesh=mesh, in_specs=in_specs, out_specs=out_specs, check_vma=False)
```

time: 857 us -> 169 us (0.20); the launches traced: 847 us -> 169 us
  waiting for transfers between devices: 454 us -> 0 us
  blocking collectives: 345 us -> 0 us
  Pallas kernels: 0 us -> 163 us
  matrix products: 19 us -> 0 us
  between operations: 14.3 us -> 0.68 us
    psum x2 -> x0, waiting for transfers between devices: 302 us -> none  [the longest x1 166 us: body(): class_g = lax.psum(partial_value, 'tpl')]
    psum x2 -> x0, blocking collectives: 261 us -> none  [the longest x1 195 us: body(): totals = lax.psum(jnp.sum(exp_scores, axis=0), ('img', 'cls'))]
    pallas_call x0 -> x1, Pallas kernels: none -> 163 us  [body(): pl.pallas_call(kernel, out_shape=(jax.ShapeDtypeStruct((256, 1280), BF),...]
    all_gather x3 -> x0, waiting for transfers between devices: 102 us -> none  [the longest x1 43.4 us: body(): full_proj = lax.all_gather(wide_proj, 'img', axis=0, tiled=True)]
    all_gather x2 -> x0, blocking collectives: 56.3 us -> none  [the longest x1 47 us: body(): wide_proj = lax.all_gather(projection, 'cls', axis=1, tiled=True)]
    unnamed x7 -> x0, waiting for transfers between devices: 49.6 us -> none
    all_to_all x1 -> x0, blocking collectives: 27.5 us -> none  [body(): lax.all_to_all(flat_tpl, 'img', split_axis=1, concat_axis=0, tiled=True)]
    dot_general x5 -> x0, matrix products: 19 us -> none  [the longest x1 4.33 us: body(): jnp.einsum('cd,nd->cn', class_b, all_img, preferred_element_type=jnp.floa...]
  transfers between devices with their start and end apart: 6 -> 0, of which waited for: 6 -> 0; matrix products, arithmetic and copies ran while one was open for 1% -> 0% of each run, Pallas kernels for 0% -> 0%
where the time goes in v1:
time: 169 us
  Pallas kernels  163 us (96%)
  local copies, waits for them, and re-layouts  4.79 us (3%)
    pallas_call x1, Pallas kernels, body(): pl.pallas_call(kernel, out_shape=(jax.ShapeDtypeStruct((256, 1280), BF),...  163 us
    unnamed x10, local copies, waits for them, and re-layouts  3.39 us

profile of v1, /device:TPU:1, one launch (start us, length us, event | category | flops | bytes accessed | tf_op | source)
XLA Modules:
  0.0 168.5 jit_solution(644375455475310637)
XLA Ops:
  0.6 0.0 copy-start.3
  0.6 0.7 copy-done.3
  1.3 0.0 copy-start.2
  1.3 1.4 copy.6
  2.7 0.0 copy-start
  2.7 0.0 copy-start.1
  2.7 0.0 copy-done.2
  2.8 1.0 copy-done
  3.8 0.2 copy-done.1
  4.0 163.1 %shard_map.59 = (bf16[256,1280]{1,0:T(8,128)(2,1)S(1)}, f32[160,160]{1,0:T(8,128)S(1)}) custom-call(bf16[256,1280]{1,0:T(8,128)(2,1)S(1)} %copy-done.1, s32[8,256]{1,0:T(8,128)S(1)} %broadcast_in_dim.2.labels, bf16[256,1280]{1,0:T(8,128)(2,1)S(1)} %bitcast.9, bf16[2,4,160,256]{3,2,1,0:T(8,128)(2,1)S(1)} %bitcast.10, bf16[160,160]{1,0:T(8,128)(2,1)S(1)} %copy-done.2), custom_call_target="tpu_custom_call" | custom-call | tf_op jit(solution)/shard_map/pallas_call | solution.py:288
  167.0 0.8 copy.12
  167.9 0.7 copy.13
  (2 shorter events, 0.0 us)
Async XLA Ops:
  0.6 0.7 copy-start.3
  1.3 1.4 copy-start.2
  2.7 1.1 copy-start
  2.7 1.3 copy-start.1

commit v2 on v1

v2 whole, which is shorter than its diff:
```python
import jax
import jax.numpy as jnp
from jax import lax
from jax.experimental import pallas as pl
from jax.experimental.pallas import tpu as pltpu
from jax.sharding import PartitionSpec as P

SCALE = 50.0
EPS = 1e-06
TPL = 32
MESH = pl.DeviceIdType.MESH
BF = jnp.bfloat16
F32 = jnp.float32
PLANE = [(a, b) for a in range(4) for b in range(4) if (a, b) != (0, 0)]
RING = (4, -4, 3, -3, 2, -2, 1, -1)


def inv_norm(v):
    return lax.rsqrt(jnp.sum(v * v, axis=-1, keepdims=True) + EPS)


def device(x, k, y, zh, zl):
    return (x * 2 + k, zl, zh * 4 + y)


class Copies:
    def __init__(self, send, recv):
        self.send, self.recv, self.used = send, recv, 0
        self.open = []

    def __call__(self, src, dst, to):
        n = self.used
        self.used += 1
        cp = pltpu.make_async_remote_copy(
            src_ref=src, dst_ref=dst, send_sem=self.send.at[n], recv_sem=self.recv.at[n],
            device_id=to, device_id_type=MESH)
        cp.start()
        self.open.append(cp)
        return cp

    def finish(self):
        for cp in self.open:
            cp.wait_send()


N_COPIES = 130
NEAR = (4, 3, -3, 2, -2, 1, -1)


def kernel(images, labels, tpl, proj, gt_out, gp_out,
           wf, pw, zb, pf, tt, zbuf, rzbuf, s_send, s_recv, c_send, c_recv, mbuf, cb, img, lab,
           ebuf, e_send, e_one, e_two, e_recv, gbuf, cg_send, cg_recv, f_send, f_recv, gs, gz, gx,
           hs, hr, h2, h2r, rs, w_recv, h_send, h_recv, hp, hy,
           send_sem, recv_sem, z_send, z_recv, w_send, w_recv_sem, y_send, y_recv):
    i = lax.axis_index("img")
    c = lax.axis_index("cls")
    t = lax.axis_index("tpl")
    x, k, y, zh = i // 2, i % 2, t % 4, t // 4
    z = zh * 8 + c
    other = 1 - k
    row_core, col_core = y // 2, c // 4

    def at_plane(dx, dy):
        return (x + dx) % 4, (y + dy) % 4

    def to_plane(dx, dy):
        px, py = at_plane(dx, dy)
        return device(px, k, py, zh, c)

    def to_z(n, core):
        n = (n + 16) % 16
        return device(x, core, y, n // 8, n % 8)

    def to_first(d):
        return device((x + d * other) % 4, k, (y + d * k) % 4, zh, c)

    def to_second(d):
        return device((x + d * k) % 4, k, (y + d * other) % 4, zh, c)

    def place(first, second):
        return first * other + second * k, second * other + first * k

    first, second = place(x, y)
    sibling = device(x, other, y, zh, c)
    across = device(x, k, y, 1 - zh, c)

    barrier = pltpu.get_barrier_semaphore()
    peers = [to_plane(dx, dy) for dx, dy in PLANE]
    peers += [to_z(z + d, k) for d in range(1, 16)]
    peers += [to_z(z + d, other) for d in RING]
    peers += [device(x, other, (y + d) % 4, zh, c) for d in range(4)]
    for peer in peers:
        pl.semaphore_signal(barrier, inc=1, device_id=peer, device_id_type=MESH)

    copy = Copies(send_sem, recv_sem)

    wf[...] = jnp.zeros_like(wf)
    wf[:, 0:160] = proj[pl.ds(pl.multiple_of(80 * (y % 2), 16), 80), :].astype(F32)
    pw[...] = pltpu.roll(wf[...], 32 * (c % 4), 1).astype(BF)

    pl.semaphore_wait(barrier, len(peers))

    def col_copy(n, to):
        return pltpu.make_async_remote_copy(
            src_ref=pw, dst_ref=zb.at[c % 4], send_sem=z_send.at[n], recv_sem=z_recv.at[c % 4],
            device_id=to, device_id_type=MESH)

    @pl.when(k == row_core)
    def _():
        for n, d in enumerate(NEAR):
            col_copy(n, to_z(z + d, col_core)).start()

        @pl.when(k != col_core)
        def _():
            col_copy(7, sibling).start()

        @pl.when(k == col_core)
        def _():
            zb[c % 4] = pw[...]

    tt[k] = tpl[...].T.reshape(4, 4, 80, 256)
    img_f = images[...].astype(F32)
    img[k] = (img_f * inv_norm(img_f)).astype(BF)
    lab[k] = labels[...]
    to_img = copy(img.at[k], img.at[k], sibling)
    to_lab = copy(lab.at[k], lab.at[k], sibling)
    to_tx = copy(tt.at[k], tt.at[k], sibling)

    for j in range(4):
        @pl.when(jnp.logical_or(4 * k + j != c, k != row_core))
        def _():
            pltpu.make_async_remote_copy(
                src_ref=pw, dst_ref=zb.at[j], send_sem=z_send.at[0], recv_sem=z_recv.at[j],
                device_id=sibling, device_id_type=MESH).wait_recv()

    @pl.when(k == row_core)
    def _():
        for n, d in enumerate(NEAR):
            col_copy(n, to_z(z + d, col_core)).wait_send()

        @pl.when(k != col_core)
        def _():
            col_copy(7, sibling).wait_send()
    tiles = [
        zb[0, :, 0:128],
        zb[0, :, 128:256] + zb[1, :, 0:128],
        zb[1, :, 128:256] + zb[2, :, 0:128],
        zb[2, :, 128:256] + zb[3, :, 0:128],
        zb[3, :, 128:256],
    ]
    for j, tile in enumerate(tiles):
        pf[k, x, y, :, j * 128:(j + 1) * 128] = tile

    def piece(d1, d2):
        px, py = place((first + d1) % 4, (second + d2) % 4)
        return pf.at[k, px, py]

    def send(d1, d2, to):
        return copy(piece(d1, d2), piece(d1, d2), to)

    shared = []
    ahead = {d: send(0, 0, to_first(d)) for d in (1, 3, 2)}
    up, down = {}, {}
    for d1 in (0, 3, 1, 2):
        if d1:
            ahead[(4 - d1) % 4].wait_recv()
        up[d1] = send(d1, 0, to_second(1))
        down[d1] = send(d1, 0, to_second(3))
        shared.append(send(d1, 0, sibling))
    far = {}
    for d1 in (0, 3, 1, 2):
        up[d1].wait_recv()
        if d1 in (0, 3):
            far[d1] = send(d1, 3, to_second(1))
        down[d1].wait_recv()
        if d1 in (1, 2):
            far[d1] = send(d1, 1, to_second(3))
        shared.append(send(d1, 3, sibling))
        shared.append(send(d1, 1, sibling))
    for d1 in (0, 1, 3, 2):
        far[d1].wait_recv()
        shared.append(send(d1, 2, sibling))
    for cp in shared:
        cp.wait_recv()

    for h in range(2):
        zbuf[:, h * 640:(h + 1) * 640] = jnp.dot(
            tpl[...], pf[h].reshape(1280, 640), preferred_element_type=F32)
    rz = inv_norm(zbuf[...])
    rzbuf[...] = rz
    zbuf[...] = zbuf[...] * rz
    total = zbuf[0:64] + zbuf[64:128] + zbuf[128:192] + zbuf[192:256]
    s_send[...] = total.astype(BF).reshape(4, 16, 1280)

    got = [copy(s_send.at[(y + d) % 4], s_recv.at[d - 1], to_plane(0, d)) for d in (2, 1, 3)]
    for cp in got:
        cp.wait_recv()
    own = s_send[y].astype(F32)
    for d in range(3):
        own = own + s_recv[d].astype(F32)
    c_send[...] = own.astype(BF)
    copy(c_send, c_recv, across).wait_recv()
    mbuf[x, y] = ((c_send[...].astype(F32) + c_recv[...].astype(F32)) / TPL).astype(BF)

    got = [copy(mbuf.at[x, y], mbuf.at[x, y], to_plane(dx, dy)) for dx, dy in PLANE]
    to_img.wait_recv()
    to_lab.wait_recv()
    to_tx.wait_recv()
    for cp in got:
        cp.wait_recv()

    mean = mbuf[...].reshape(256, 1280).astype(F32)
    cb[...] = (mean * inv_norm(mean)).astype(BF)
    for s in range(2):
        sc = lax.dot_general(cb[...], img[s], (((1,), (1,)), ((), ())), preferred_element_type=F32)
        ebuf[:, s * 256:(s + 1) * 256] = jnp.exp(SCALE * sc)
    e_send[...] = jnp.sum(ebuf[...], axis=0, keepdims=True)
    copy(e_send, e_one, sibling).wait_recv()
    e_two[...] = e_send[...] + e_one[...]
    got = [copy(e_two, e_recv.at[d - 1], device(x, k, y, zh, (c + d) % 8)) for d in range(1, 8)]
    row = lax.broadcasted_iota(jnp.int32, (256, 1), 0)
    ids = (c * 8 + (row // 64) * 2 + k) * 64 + row % 64
    for cp in got:
        cp.wait_recv()
    tot = e_two[...]
    for d in range(7):
        tot = tot + e_recv[d]
    inv = 1.0 / tot
    for s in range(2):
        part = slice(s * 256, (s + 1) * 256)
        hot = (lab[s, 0:1, :] == ids).astype(F32)
        gbuf[:, part] = (ebuf[:, part] * inv[:, part] - hot).astype(BF)

    def class_grad(n, _):
        o = pl.ds(pl.multiple_of(n * 256, 256), 256)
        v = jnp.dot(gbuf[...], img[:, :, o].reshape(512, 256), preferred_element_type=F32)
        cg_send[:, :, :, o] = (SCALE * v).astype(BF).reshape(4, 4, 16, 256)
        return 0
    lax.fori_loop(0, 5, class_grad, 0)

    got = []
    for n, (dx, dy) in enumerate(PLANE):
        px, py = at_plane(dx, dy)
        got.append(copy(cg_send.at[px, py], cg_recv.at[n], to_plane(dx, dy)))
    for cp in got:
        cp.wait_recv()
    own = cg_send[x, y].astype(F32)
    for n in range(15):
        own = own + cg_recv[n].astype(F32)
    f_send[...] = own.astype(BF)
    copy(f_send, f_recv, across).wait_recv()
    gs[y] = (f_send[...].astype(F32) + f_recv[...].astype(F32)).astype(BF)
    got = [copy(gs.at[y], gs.at[y], to_plane(0, d)) for d in (2, 1, 3)]
    mean = mbuf[x].reshape(64, 1280).astype(F32)
    rn = inv_norm(mean)
    class_w = mean * rn
    for cp in got:
        cp.wait_recv()

    class_g = gs[...].reshape(64, 1280).astype(F32)
    dot_wg = jnp.sum(class_w * class_g, axis=1, keepdims=True)
    per_u = (class_g - class_w * dot_wg) * rn / TPL
    for n in range(4):
        rows_n = slice(n * 64, (n + 1) * 64)
        u = zbuf[rows_n]
        inner = jnp.sum(u * per_u, axis=1, keepdims=True)
        gz[rows_n] = ((per_u - u * inner) * rzbuf[rows_n]).astype(BF)

    def half(core):
        return pl.ds(pl.multiple_of(640 * core, 128), 640)

    copy(gz.at[:, half(other)], gx, sibling).wait_recv()

    g_own, g_other = gz[:, half(k)], gx[...]
    got = {}
    for d in (2, 1, 3, 0):
        j = (first + d) % 4
        spots = [place(j, m) for m in range(4)]
        lhs = jnp.concatenate([tt[k, px, py] for px, py in spots], axis=0)
        v = jnp.dot(lhs, g_own, preferred_element_type=F32)
        lhs = jnp.concatenate([tt[other, px, py] for px, py in spots], axis=0)
        v = v + jnp.dot(lhs, g_other, preferred_element_type=F32)
        hs[j] = v.astype(BF).reshape(4, 80, 640)
        if d:
            got[d] = copy(hs.at[j], hr.at[d - 1], to_first(d))

    for m in range(4):
        v = 0.0
        for h in range(2):
            w = pf[h, m].reshape(320, 640)
            v = v + lax.dot_general(
                gz[:, h * 640:(h + 1) * 640], w, (((1,), (1,)), ((), ())), preferred_element_type=F32)
        gt_out[:, m * 320:(m + 1) * 320] = v.astype(BF)

    for d in (1, 3, 2):
        got[d].wait_recv()
    for m in range(4):
        own = hs[first, m].astype(F32)
        for d in range(3):
            own = own + hr[d, m].astype(F32)
        h2[m] = own.astype(BF)
    got = [copy(h2.at[(second + d) % 4], h2r.at[d - 1], to_second(d)) for d in (2, 1, 3)]
    for cp in got:
        cp.wait_recv()
    own = h2[second].astype(F32)
    for d in range(3):
        own = own + h2r[d].astype(F32)
    rs[...] = own.astype(BF)

    def block_copy(j):
        ahead = (4 * k + j - c + 8) % 8
        near = z + ahead - 8 * (ahead // 5)
        slot = (ahead + 6) % 7
        return ahead, pltpu.make_async_remote_copy(
            src_ref=rs.at[:, pl.ds(128 * j, 256)], dst_ref=w_recv.at[slot],
            send_sem=w_send.at[j], recv_sem=w_recv_sem.at[slot],
            device_id=to_z(near, k), device_id_type=MESH)

    for j in range(4):
        ahead_j, cp = block_copy(j)

        @pl.when(ahead_j != 0)
        def _():
            cp.start()

    def final_copy(n, core, py):
        return pltpu.make_async_remote_copy(
            src_ref=hp, dst_ref=hy.at[y % 2], send_sem=y_send.at[n], recv_sem=y_recv.at[y % 2],
            device_id=device(x, core, py, zh, c), device_id_type=MESH)

    @pl.when(k == col_core)
    def _():
        own = rs[:, pl.ds(pl.multiple_of(128 * (c % 4), 128), 256)].astype(F32)
        for n in range(7):
            pltpu.make_async_remote_copy(
                src_ref=h_send, dst_ref=w_recv.at[n], send_sem=w_send.at[0], recv_sem=w_recv_sem.at[n],
                device_id=sibling, device_id_type=MESH).wait_recv()
            own = own + w_recv[n].astype(F32)
        h_send[...] = own.astype(BF)
        cp = pltpu.make_async_remote_copy(
            src_ref=h_send, dst_ref=h_recv, send_sem=w_send.at[4], recv_sem=w_recv_sem.at[7],
            device_id=across, device_id_type=MESH)
        cp.start()
        cp.wait()
        whole = h_send[...].astype(F32) + h_recv[...].astype(F32)
        hp[...] = pltpu.roll(whole, (256 - 32 * (c % 4)) % 256, 1).astype(BF)
        for d in (2, 1, 3):
            final_copy(d, row_core, (y + d) % 4).start()

        @pl.when(k != row_core)
        def _():
            final_copy(0, row_core, y).start()

        @pl.when(k == row_core)
        def _():
            hy[y % 2] = hp[...]

    for n in range(2):
        @pl.when(jnp.logical_or(2 * k + n != y, k != col_core))
        def _():
            pltpu.make_async_remote_copy(
                src_ref=hp, dst_ref=hy.at[n], send_sem=y_send.at[0], recv_sem=y_recv.at[n],
                device_id=sibling, device_id_type=MESH).wait_recv()
        gp_out[80 * n:80 * n + 80] = hy[n, :, 0:160].astype(F32)

    for j in range(4):
        ahead_j, cp = block_copy(j)

        @pl.when(ahead_j != 0)
        def _():
            cp.wait_send()

    @pl.when(k == col_core)
    def _():
        for d in (2, 1, 3):
            final_copy(d, row_core, (y + d) % 4).wait_send()

        @pl.when(k != row_core)
        def _():
            final_copy(0, row_core, y).wait_send()
    copy.finish()


def body(images, labels, templates, projection):
    flat = templates.reshape(256, 1280)
    lab = jnp.broadcast_to(labels.reshape(1, 256), (8, 256))
    vm = pl.BlockSpec(memory_space=pltpu.VMEM)
    scratch = [
        ((80, 256), F32), ((80, 256), BF), ((4, 80, 256), BF), ((2, 4, 4, 80, 640), BF),
        ((2, 4, 4, 80, 256), BF), ((256, 1280), F32), ((256, 1), F32),
        ((4, 16, 1280), BF), ((3, 16, 1280), BF), ((16, 1280), BF), ((16, 1280), BF),
        ((4, 4, 16, 1280), BF), ((256, 1280), BF), ((2, 256, 1280), BF), ((2, 8, 256), jnp.int32),
        ((256, 512), F32), ((1, 512), F32), ((1, 512), F32), ((1, 512), F32), ((7, 1, 512), F32),
        ((256, 512), BF), ((4, 4, 16, 1280), BF), ((15, 16, 1280), BF), ((16, 1280), BF), ((16, 1280), BF),
        ((4, 16, 1280), BF), ((256, 1280), BF), ((256, 640), BF),
        ((4, 4, 80, 640), BF), ((3, 4, 80, 640), BF), ((4, 80, 640), BF), ((3, 80, 640), BF),
        ((80, 640), BF), ((7, 80, 256), BF), ((80, 256), BF), ((80, 256), BF), ((80, 256), BF),
        ((2, 80, 256), BF),
    ]
    sems = (N_COPIES, N_COPIES, 8, 4, 5, 8, 4, 2)
    gt, gp = pl.pallas_call(
        kernel,
        out_shape=(jax.ShapeDtypeStruct((256, 1280), BF), jax.ShapeDtypeStruct((160, 160), F32)),
        in_specs=[vm] * 4,
        out_specs=(vm, vm),
        scratch_shapes=[pltpu.VMEM(s, d) for s, d in scratch]
        + [pltpu.SemaphoreType.DMA((n,)) for n in sems],
        compiler_params=pltpu.CompilerParams(
            collective_id=0, has_side_effects=True, vmem_limit_bytes=50 << 20),
    )(images, lab, flat, projection)
    return gt.reshape(templates.shape), gp


def solution(mesh):
    in_specs = (
        P(("img", "tpl"), None),
        P(("img", "tpl")),
        P("tpl", ("cls", "img"), None),
        P("img", "cls"),
    )
    out_specs = (P("tpl", ("cls", "img"), None), P("img", "cls"))
    return jax.shard_map(body, mesh=mesh, in_specs=in_specs, out_specs=out_specs, check_vma=False)
```

time: 169 us -> 140 us (0.83)
  Pallas kernels: 163 us -> 134 us
    pallas_call x1, Pallas kernels: 163 us -> 134 us  [body(): pl.pallas_call(kernel, out_shape=(jax.ShapeDtypeStruct((256, 1280), BF),...]
    unnamed x10, local copies, waits for them, and re-layouts: 3.39 us -> 5.24 us
where the time goes in v2:
time: 140 us; the launch traced here: 139 us
  Pallas kernels  134 us (96%)
  local copies, waits for them, and re-layouts  5.24 us (4%)
    pallas_call x1, Pallas kernels, body(): pl.pallas_call(kernel, out_shape=(jax.ShapeDtypeStruct((256, 1280), BF),...  134 us
    unnamed x10, local copies, waits for them, and re-layouts  5.24 us

profile of v2, /device:TPU:1, one launch (start us, length us, event | category | flops | bytes accessed | tf_op | source)
XLA Modules:
  0.0 139.4 jit_solution(12632252996273450063)
XLA Ops:
  0.6 0.0 copy-start.3
  0.6 0.7 copy-done.3
  1.3 0.0 copy-start
  1.3 1.1 copy-done
  2.4 0.0 copy-start.1
  2.4 1.1 copy-done.1
  3.5 0.0 copy-start.2
  3.5 0.9 copy-done.2
  4.4 133.5 %shard_map.59 = (bf16[256,1280]{1,0:T(8,128)(2,1)S(1)}, f32[160,160]{1,0:T(8,128)S(1)}) custom-call(bf16[256,1280]{1,0:T(8,128)(2,1)S(1)} %copy-done, s32[8,256]{1,0:T(8,128)S(1)} %broadcast_in_dim.2.labels, bf16[256,1280]{1,0:T(8,128)(2,1)S(1)} %bitcast.2, bf16[160,160]{1,0:T(8,128)(2,1)S(1)} %copy-done.2), custom_call_target="tpu_custom_call" | custom-call | tf_op jit(solution)/shard_map/pallas_call | solution.py:401
  137.9 0.8 copy.8
  138.7 0.7 copy.9
  (1 shorter events, 0.0 us)
Async XLA Ops:
  0.6 0.7 copy-start.3
  1.3 1.1 copy-start
  2.4 1.1 copy-start.1
  3.5 0.9 copy-start.2

commit v3 on v2

--- a/solution.py
+++ b/solution.py
@@ -43,15 +43,15 @@
             cp.wait_send()
 
 
-N_COPIES = 130
+N_COPIES = 190
 NEAR = (4, 3, -3, 2, -2, 1, -1)
 
 
-def kernel(images, labels, tpl, proj, gt_out, gp_out,
-           wf, pw, zb, pf, tt, zbuf, rzbuf, s_send, s_recv, c_send, c_recv, mbuf, cb, img, lab,
-           ebuf, e_send, e_one, e_two, e_recv, gbuf, cg_send, cg_recv, f_send, f_recv, gs, gz, gx,
+def kernel(images_in, labels_in, tpl_in, proj_in, gt_out, gp_out,
+           images, tpl, proj, wf, pw, zb, pf, tt, zbuf, rzbuf, s_send, s_recv, c_send, c_recv, mbuf, mo, cb,
+           img, lab, ebuf, e_send, e_recv, gbuf, cg_send, cg_recv, f2, f2r, f_send, f_recv, gs, gz, gx,
            hs, hr, h2, h2r, rs, w_recv, h_send, h_recv, hp, hy,
-           send_sem, recv_sem, z_send, z_recv, w_send, w_recv_sem, y_send, y_recv):
+           load_sem, send_sem, recv_sem, z_send, z_recv, w_send, w_recv_sem, y_send, y_recv):
     i = lax.axis_index("img")
     c = lax.axis_index("cls")
     t = lax.axis_index("tpl")
@@ -86,15 +86,24 @@
 
     barrier = pltpu.get_barrier_semaphore()
     peers = [to_plane(dx, dy) for dx, dy in PLANE]
-    peers += [to_z(z + d, k) for d in range(1, 16)]
+    peers += [to_z(z + d, k) for d in RING]
     peers += [to_z(z + d, other) for d in RING]
     peers += [device(x, other, (y + d) % 4, zh, c) for d in range(4)]
     for peer in peers:
         pl.semaphore_signal(barrier, inc=1, device_id=peer, device_id_type=MESH)
 
+    loads = [
+        pltpu.make_async_copy(src, dst, load_sem.at[n])
+        for n, (src, dst) in enumerate(
+            ((proj_in, proj), (tpl_in, tpl), (images_in, images), (labels_in, lab.at[k])))
+    ]
+    for load in loads:
+        load.start()
+
     copy = Copies(send_sem, recv_sem)
 
     wf[...] = jnp.zeros_like(wf)
+    loads[0].wait()
     wf[:, 0:160] = proj[pl.ds(pl.multiple_of(80 * (y % 2), 16), 80), :].astype(F32)
     pw[...] = pltpu.roll(wf[...], 32 * (c % 4), 1).astype(BF)
 
@@ -118,10 +127,11 @@
         def _():
             zb[c % 4] = pw[...]
 
+    for load in loads[1:]:
+        load.wait()
     tt[k] = tpl[...].T.reshape(4, 4, 80, 256)
     img_f = images[...].astype(F32)
     img[k] = (img_f * inv_norm(img_f)).astype(BF)
-    lab[k] = labels[...]
     to_img = copy(img.at[k], img.at[k], sibling)
     to_lab = copy(lab.at[k], lab.at[k], sibling)
     to_tx = copy(tt.at[k], tt.at[k], sibling)
@@ -192,74 +202,115 @@
     total = zbuf[0:64] + zbuf[64:128] + zbuf[128:192] + zbuf[192:256]
     s_send[...] = total.astype(BF).reshape(4, 16, 1280)
 
-    got = [copy(s_send.at[(y + d) % 4], s_recv.at[d - 1], to_plane(0, d)) for d in (2, 1, 3)]
-    for cp in got:
-        cp.wait_recv()
-    own = s_send[y].astype(F32)
-    for d in range(3):
-        own = own + s_recv[d].astype(F32)
-    c_send[...] = own.astype(BF)
-    copy(c_send, c_recv, across).wait_recv()
-    mbuf[x, y] = ((c_send[...].astype(F32) + c_recv[...].astype(F32)) / TPL).astype(BF)
-
-    got = [copy(mbuf.at[x, y], mbuf.at[x, y], to_plane(dx, dy)) for dx, dy in PLANE]
+    halves = [pl.ds(0, 640), pl.ds(640, 640)]
+    got = [
+        [copy(s_send.at[(y + d) % 4, :, h], s_recv.at[d - 1, :, h], to_plane(0, d)) for d in (2, 1, 3)]
+        for h in halves
+    ]
+    four = []
+    for n, h in enumerate(halves):
+        for cp in got[n]:
+            cp.wait_recv()
+        own = s_send[y, :, h].astype(F32)
+        for d in range(3):
+            own = own + s_recv[d, :, h].astype(F32)
+        c_send[:, h] = own.astype(BF)
+        four.append([
+            copy(c_send.at[:, h], c_recv.at[0, :, h], to_z(z + 4, k)),
+            copy(c_send.at[:, h], c_recv.at[1, :, h], to_z(z - 4, k))])
+
+    def mean_piece(d1, h):
+        px, py = place((first + d1) % 4, second)
+        return mbuf.at[px, py, :, h]
+
+    ahead, wide, back = [], [], []
+    for n, h in enumerate(halves):
+        for cp in four[n]:
+            cp.wait_recv()
+        mbuf[x, y, :, h] = ((c_recv[0, :, h].astype(F32) + c_recv[1, :, h].astype(F32)) / TPL).astype(BF)
+        src = mean_piece(0, h)
+        ahead.append({d: copy(src, src, to_first(d)) for d in (2, 1, 3)})
+        wide += [copy(src, src, to_second(d)) for d in (2, 1, 3)]
+        back.append(copy(src, mo.at[:, h], to_z(z + 4 - 8 * n, k)))
+    for n, h in enumerate(halves):
+        for d in (3, 1, 2):
+            ahead[n][d].wait_recv()
+            src = mean_piece(4 - d, h)
+            wide += [copy(src, src, to_second(e)) for e in (2, 1, 3)]
     to_img.wait_recv()
     to_lab.wait_recv()
     to_tx.wait_recv()
-    for cp in got:
-        cp.wait_recv()
-
+    for cp in wide:
+        cp.wait_recv()
     mean = mbuf[...].reshape(256, 1280).astype(F32)
     cb[...] = (mean * inv_norm(mean)).astype(BF)
     for s in range(2):
         sc = lax.dot_general(cb[...], img[s], (((1,), (1,)), ((), ())), preferred_element_type=F32)
         ebuf[:, s * 256:(s + 1) * 256] = jnp.exp(SCALE * sc)
     e_send[...] = jnp.sum(ebuf[...], axis=0, keepdims=True)
-    copy(e_send, e_one, sibling).wait_recv()
-    e_two[...] = e_send[...] + e_one[...]
-    got = [copy(e_two, e_recv.at[d - 1], device(x, k, y, zh, (c + d) % 8)) for d in range(1, 8)]
+    got = []
+    for d in (4, 3, 5, 2, 6, 1, 7):
+        for core in (k, other):
+            got.append(copy(e_send, e_recv.at[len(got)], device(x, core, y, zh, (c + d) % 8)))
+    got.append(copy(e_send, e_recv.at[14], sibling))
     row = lax.broadcasted_iota(jnp.int32, (256, 1), 0)
-    ids = (c * 8 + (row // 64) * 2 + k) * 64 + row % 64
+    ids = (((c + 4) % 8) * 8 + (row // 64) * 2 + k) * 64 + row % 64
     for cp in got:
         cp.wait_recv()
-    tot = e_two[...]
-    for d in range(7):
-        tot = tot + e_recv[d]
+    tot = e_send[...]
+    for n in range(15):
+        tot = tot + e_recv[n]
     inv = 1.0 / tot
     for s in range(2):
         part = slice(s * 256, (s + 1) * 256)
         hot = (lab[s, 0:1, :] == ids).astype(F32)
         gbuf[:, part] = (ebuf[:, part] * inv[:, part] - hot).astype(BF)
 
-    def class_grad(n, _):
-        o = pl.ds(pl.multiple_of(n * 256, 256), 256)
-        v = jnp.dot(gbuf[...], img[:, :, o].reshape(512, 256), preferred_element_type=F32)
-        cg_send[:, :, :, o] = (SCALE * v).astype(BF).reshape(4, 4, 16, 256)
-        return 0
-    lax.fori_loop(0, 5, class_grad, 0)
-
     got = []
-    for n, (dx, dy) in enumerate(PLANE):
-        px, py = at_plane(dx, dy)
-        got.append(copy(cg_send.at[px, py], cg_recv.at[n], to_plane(dx, dy)))
-    for cp in got:
-        cp.wait_recv()
-    own = cg_send[x, y].astype(F32)
-    for n in range(15):
-        own = own + cg_recv[n].astype(F32)
-    f_send[...] = own.astype(BF)
-    copy(f_send, f_recv, across).wait_recv()
-    gs[y] = (f_send[...].astype(F32) + f_recv[...].astype(F32)).astype(BF)
-    got = [copy(gs.at[y], gs.at[y], to_plane(0, d)) for d in (2, 1, 3)]
-    mean = mbuf[x].reshape(64, 1280).astype(F32)
+    for n, h in enumerate(halves):
+        v = jnp.dot(gbuf[...], img[:, :, h].reshape(512, 640), preferred_element_type=F32)
+        cg_send[n] = (SCALE * v).astype(BF).reshape(4, 4, 16, 640)
+        got.append([])
+        for d in (2, 1, 3):
+            for m in range(4):
+                px, py = place((first + d) % 4, m)
+                got[n].append(copy(cg_send.at[n, px, py], cg_recv.at[n, d - 1, m], to_first(d)))
+    step = []
+    for n in range(2):
+        for cp in got[n]:
+            cp.wait_recv()
+        for m in range(4):
+            px, py = place(first, m)
+            own = cg_send[n, px, py].astype(F32)
+            for d in range(3):
+                own = own + cg_recv[n, d, m].astype(F32)
+            f2[n, m] = own.astype(BF)
+        step.append([
+            copy(f2.at[n, (second + d) % 4], f2r.at[n, d - 1], to_second(d)) for d in (2, 1, 3)])
+    four = []
+    for n, h in enumerate(halves):
+        for cp in step[n]:
+            cp.wait_recv()
+        own = f2[n, second].astype(F32)
+        for d in range(3):
+            own = own + f2r[n, d].astype(F32)
+        f_send[:, h] = own.astype(BF)
+        four += [
+            copy(f_send.at[:, h], f_recv.at[0, :, h], to_z(z + 4, k)),
+            copy(f_send.at[:, h], f_recv.at[1, :, h], to_z(z - 4, k))]
+    for cp in back:
+        cp.wait_recv()
+    mean = mo[...].astype(F32)
     rn = inv_norm(mean)
     class_w = mean * rn
-    for cp in got:
-        cp.wait_recv()
-
-    class_g = gs[...].reshape(64, 1280).astype(F32)
+    for cp in four:
+        cp.wait_recv()
+    class_g = f_recv[0].astype(F32) + f_recv[1].astype(F32)
     dot_wg = jnp.sum(class_w * class_g, axis=1, keepdims=True)
-    per_u = (class_g - class_w * dot_wg) * rn / TPL
+    gs[y] = ((class_g - class_w * dot_wg) * rn / TPL).astype(BF)
+    for cp in [copy(gs.at[y], gs.at[y], to_plane(0, d)) for d in (2, 1, 3)]:
+        cp.wait_recv()
+    per_u = gs[...].reshape(64, 1280).astype(F32)
     for n in range(4):
         rows_n = slice(n * 64, (n + 1) * 64)
         u = zbuf[rows_n]
@@ -383,31 +434,33 @@
 
 def body(images, labels, templates, projection):
     flat = templates.reshape(256, 1280)
-    lab = jnp.broadcast_to(labels.reshape(1, 256), (8, 256))
     vm = pl.BlockSpec(memory_space=pltpu.VMEM)
+    hbm = pl.BlockSpec(memory_space=pl.ANY)
     scratch = [
+        ((256, 1280), BF), ((256, 1280), BF), ((160, 160), BF),
         ((80, 256), F32), ((80, 256), BF), ((4, 80, 256), BF), ((2, 4, 4, 80, 640), BF),
         ((2, 4, 4, 80, 256), BF), ((256, 1280), F32), ((256, 1), F32),
-        ((4, 16, 1280), BF), ((3, 16, 1280), BF), ((16, 1280), BF), ((16, 1280), BF),
-        ((4, 4, 16, 1280), BF), ((256, 1280), BF), ((2, 256, 1280), BF), ((2, 8, 256), jnp.int32),
-        ((256, 512), F32), ((1, 512), F32), ((1, 512), F32), ((1, 512), F32), ((7, 1, 512), F32),
-        ((256, 512), BF), ((4, 4, 16, 1280), BF), ((15, 16, 1280), BF), ((16, 1280), BF), ((16, 1280), BF),
+        ((4, 16, 1280), BF), ((3, 16, 1280), BF), ((16, 1280), BF), ((2, 16, 1280), BF),
+        ((4, 4, 16, 1280), BF), ((16, 1280), BF), ((256, 1280), BF), ((2, 256, 1280), BF),
+        ((2, 1, 256), jnp.int32), ((256, 512), F32), ((1, 512), F32), ((15, 1, 512), F32),
+        ((256, 512), BF), ((2, 4, 4, 16, 640), BF), ((2, 3, 4, 16, 640), BF), ((2, 4, 16, 640), BF),
+        ((2, 3, 16, 640), BF), ((16, 1280), BF), ((2, 16, 1280), BF),
         ((4, 16, 1280), BF), ((256, 1280), BF), ((256, 640), BF),
         ((4, 4, 80, 640), BF), ((3, 4, 80, 640), BF), ((4, 80, 640), BF), ((3, 80, 640), BF),
         ((80, 640), BF), ((7, 80, 256), BF), ((80, 256), BF), ((80, 256), BF), ((80, 256), BF),
         ((2, 80, 256), BF),
     ]
-    sems = (N_COPIES, N_COPIES, 8, 4, 5, 8, 4, 2)
+    sems = (4, N_COPIES, N_COPIES, 8, 4, 5, 8, 4, 2)
     gt, gp = pl.pallas_call(
         kernel,
         out_shape=(jax.ShapeDtypeStruct((256, 1280), BF), jax.ShapeDtypeStruct((160, 160), F32)),
-        in_specs=[vm] * 4,
+        in_specs=[hbm] * 4,
         out_specs=(vm, vm),
         scratch_shapes=[pltpu.VMEM(s, d) for s, d in scratch]
         + [pltpu.SemaphoreType.DMA((n,)) for n in sems],
         compiler_params=pltpu.CompilerParams(
-            collective_id=0, has_side_effects=True, vmem_limit_bytes=50 << 20),
-    )(images, lab, flat, projection)
+            collective_id=0, has_side_effects=True, vmem_limit_bytes=60 << 20),
+    )(images, labels.reshape(1, 256), flat, projection)
     return gt.reshape(templates.shape), gp
 
 

time: 140 us -> 128 us (0.914)
  Pallas kernels: 134 us -> 125 us
  local copies, waits for them, and re-layouts: 5.24 us -> 2.67 us
    pallas_call x1, Pallas kernels: 134 us -> 125 us  [body(): pl.pallas_call(kernel, out_shape=(jax.ShapeDtypeStruct((256, 1280), BF),...]
    unnamed x10 -> x4, local copies, waits for them, and re-layouts: 5.24 us -> 2.67 us
where the time goes in v3:
time: 128 us
  Pallas kernels  125 us (98%)
  local copies, waits for them, and re-layouts  2.67 us (2%)
    pallas_call x1, Pallas kernels, body(): pl.pallas_call(kernel, out_shape=(jax.ShapeDtypeStruct((256, 1280), BF),...  125 us
    unnamed x4, local copies, waits for them, and re-layouts  2.67 us

profile of v3, /device:TPU:1, one launch (start us, length us, event | category | flops | bytes accessed | tf_op | source)
XLA Modules:
  0.0 128.3 jit_solution(16695807652976263021)
XLA Ops:
  0.6 125.0 %shard_map.59 = (bf16[256,1280]{1,0:T(8,128)(2,1)}, f32[160,160]{1,0:T(8,128)}) custom-call(bf16[256,1280]{1,0:T(8,128)(2,1)} %images_in.1, s32[1,256]{1,0:T(1,128)} %bitcast.5, bf16[256,1280]{1,0:T(8,128)(2,1)} %bitcast.3, bf16[160,160]{1,0:T(8,128)(2,1)} %proj_in.1), custom_call_target="tpu_custom_call" | custom-call | tf_op jit(solution)/shard_map/pallas_call | solution.py:454
  125.7 0.0 copy-start
  125.7 2.0 %copy.8 = bf16[4,64,1280]{2,1,0:T(8,128)(2,1)} copy(bf16[4,64,1280]{2,1,0:T(8,128)(2,1)} %bitcast.4) | data formatting | bytes 1310720
  127.7 0.0 copy-done
  127.7 0.7 copy.9
Async XLA Ops:
  125.7 2.0 %copy-start = (f32[160,160]{1,0:T(8,128)S(1)}, f32[160,160]{1,0:T(8,128)}, u32[]{:S(2)}) copy-start(f32[160,160]{1,0:T(8,128)} %get-tuple-element.9) | copy-start | bytes 307204

commit v4 on v3

--- a/solution.py
+++ b/solution.py
@@ -44,14 +44,13 @@
 
 
 N_COPIES = 190
-NEAR = (4, 3, -3, 2, -2, 1, -1)
-
-
-def kernel(images_in, labels_in, tpl_in, proj_in, gt_out, gp_out,
-           images, tpl, proj, wf, pw, zb, pf, tt, zbuf, rzbuf, s_send, s_recv, c_send, c_recv, mbuf, mo, cb,
+
+
+def kernel(images_in, labels_in, tpl_in, proj_in, gt_low, gt_high, gp_out,
+           gt_out, images, tpl, proj, wf, pw, zb, pf, tt, zbuf, rzbuf, s_send, s_recv, c_send, c_recv, mbuf, mo, cb,
            img, lab, ebuf, e_send, e_recv, gbuf, cg_send, cg_recv, f2, f2r, f_send, f_recv, gs, gz, gx,
-           hs, hr, h2, h2r, rs, w_recv, h_send, h_recv, hp, hy,
-           load_sem, send_sem, recv_sem, z_send, z_recv, w_send, w_recv_sem, y_send, y_recv):
+           hs, hr, hc, h2, h2r, rs, w_recv, h_send, h_recv, hp, hy,
+           load_sem, store_sem, send_sem, recv_sem, z_send, z_recv, w_send, w_recv_sem, y_send, y_recv):
     i = lax.axis_index("img")
     c = lax.axis_index("cls")
     t = lax.axis_index("tpl")
@@ -82,7 +81,6 @@
 
     first, second = place(x, y)
     sibling = device(x, other, y, zh, c)
-    across = device(x, k, y, 1 - zh, c)
 
     barrier = pltpu.get_barrier_semaphore()
     peers = [to_plane(dx, dy) for dx, dy in PLANE]
@@ -109,19 +107,21 @@
 
     pl.semaphore_wait(barrier, len(peers))
 
-    def col_copy(n, to):
+    def col_copy(n, d, to, slot=None):
+        rows = pl.ds(0, 48) if d == 4 else pl.ds(48, 32) if d == -4 else pl.ds(0, 80)
+        slot = c % 4 if slot is None else slot
         return pltpu.make_async_remote_copy(
-            src_ref=pw, dst_ref=zb.at[c % 4], send_sem=z_send.at[n], recv_sem=z_recv.at[c % 4],
-            device_id=to, device_id_type=MESH)
+            src_ref=pw.at[rows], dst_ref=zb.at[slot, rows], send_sem=z_send.at[n],
+            recv_sem=z_recv.at[4 if d == -4 else slot], device_id=to, device_id_type=MESH)
 
     @pl.when(k == row_core)
     def _():
-        for n, d in enumerate(NEAR):
-            col_copy(n, to_z(z + d, col_core)).start()
+        for n, d in enumerate(RING):
+            col_copy(n, d, to_z(z + d, col_core)).start()
 
         @pl.when(k != col_core)
         def _():
-            col_copy(7, sibling).start()
+            col_copy(8, 0, sibling).start()
 
         @pl.when(k == col_core)
         def _():
@@ -137,20 +137,25 @@
     to_tx = copy(tt.at[k], tt.at[k], sibling)
 
     for j in range(4):
-        @pl.when(jnp.logical_or(4 * k + j != c, k != row_core))
-        def _():
-            pltpu.make_async_remote_copy(
-                src_ref=pw, dst_ref=zb.at[j], send_sem=z_send.at[0], recv_sem=z_recv.at[j],
-                device_id=sibling, device_id_type=MESH).wait_recv()
+        block = 4 * k + j
+
+        @pl.when(block == (c + 4) % 8)
+        def _():
+            col_copy(0, 4, sibling, j).wait_recv()
+            col_copy(0, -4, sibling, j).wait_recv()
+
+        @pl.when(jnp.logical_and(block != (c + 4) % 8, jnp.logical_or(block != c, k != row_core)))
+        def _():
+            col_copy(0, 0, sibling, j).wait_recv()
 
     @pl.when(k == row_core)
     def _():
-        for n, d in enumerate(NEAR):
-            col_copy(n, to_z(z + d, col_core)).wait_send()
+        for n, d in enumerate(RING):
+            col_copy(n, d, to_z(z + d, col_core)).wait_send()
 
         @pl.when(k != col_core)
         def _():
-            col_copy(7, sibling).wait_send()
+            col_copy(8, 0, sibling).wait_send()
     tiles = [
         zb[0, :, 0:128],
         zb[0, :, 128:256] + zb[1, :, 0:128],
@@ -190,12 +195,17 @@
     for d1 in (0, 1, 3, 2):
         far[d1].wait_recv()
         shared.append(send(d1, 2, sibling))
+
+    def half(core):
+        return pl.ds(pl.multiple_of(640 * core, 128), 640)
+
+    def project(core):
+        zbuf[:, half(core)] = jnp.dot(tpl[...], pf[core].reshape(1280, 640), preferred_element_type=F32)
+
+    project(k)
     for cp in shared:
         cp.wait_recv()
-
-    for h in range(2):
-        zbuf[:, h * 640:(h + 1) * 640] = jnp.dot(
-            tpl[...], pf[h].reshape(1280, 640), preferred_element_type=F32)
+    project(other)
     rz = inv_norm(zbuf[...])
     rzbuf[...] = rz
     zbuf[...] = zbuf[...] * rz
@@ -317,25 +327,30 @@
         inner = jnp.sum(u * per_u, axis=1, keepdims=True)
         gz[rows_n] = ((per_u - u * inner) * rzbuf[rows_n]).astype(BF)
 
-    def half(core):
-        return pl.ds(pl.multiple_of(640 * core, 128), 640)
-
-    copy(gz.at[:, half(other)], gx, sibling).wait_recv()
-
-    g_own, g_other = gz[:, half(k)], gx[...]
-    got = {}
+    to_gx = copy(gz.at[:, half(other)], gx, sibling)
+
+    def rows_of(core, j):
+        return jnp.concatenate([tt[core, px, py] for px, py in [place(j, m) for m in range(4)]], axis=0)
+
+    low, high = pl.ds(0, 2), pl.ds(2, 2)
+    g_own = gz[:, half(k)]
+    chunk = {d: (first + d) % 4 for d in range(4)}
     for d in (2, 1, 3, 0):
-        j = (first + d) % 4
-        spots = [place(j, m) for m in range(4)]
-        lhs = jnp.concatenate([tt[k, px, py] for px, py in spots], axis=0)
-        v = jnp.dot(lhs, g_own, preferred_element_type=F32)
-        lhs = jnp.concatenate([tt[other, px, py] for px, py in spots], axis=0)
-        v = v + jnp.dot(lhs, g_other, preferred_element_type=F32)
-        hs[j] = v.astype(BF).reshape(4, 80, 640)
-        if d:
-            got[d] = copy(hs.at[j], hr.at[d - 1], to_first(d))
-
-    for m in range(4):
+        v = jnp.dot(rows_of(k, chunk[d]), g_own, preferred_element_type=F32)
+        if d == 2:
+            to_gx.wait_recv()
+            g_other = gx[...]
+        v = v + jnp.dot(rows_of(other, chunk[d]), g_other, preferred_element_type=F32)
+        hs[chunk[d]] = v.astype(BF).reshape(4, 80, 640)
+        if d == 2:
+            via_up = copy(hs.at[chunk[2], low], hr.at[0], to_first(1))
+            via_down = copy(hs.at[chunk[2], high], hr.at[1], to_first(3))
+        elif d == 1:
+            own_up = copy(hs.at[chunk[1], high], hr.at[2], to_first(1))
+        elif d == 3:
+            own_down = copy(hs.at[chunk[3], low], hr.at[3], to_first(3))
+
+    def grad_tpl(m):
         v = 0.0
         for h in range(2):
             w = pf[h, m].reshape(320, 640)
@@ -343,13 +358,27 @@
                 gz[:, h * 640:(h + 1) * 640], w, (((1,), (1,)), ((), ())), preferred_element_type=F32)
         gt_out[:, m * 320:(m + 1) * 320] = v.astype(BF)
 
-    for d in (1, 3, 2):
-        got[d].wait_recv()
-    for m in range(4):
-        own = hs[first, m].astype(F32)
-        for d in range(3):
-            own = own + hr[d, m].astype(F32)
-        h2[m] = own.astype(BF)
+    grad_tpl(0)
+    grad_tpl(1)
+    via_up.wait_recv()
+    hc[0] = (hs[chunk[1], low].astype(F32) + hr[0].astype(F32)).astype(BF)
+    sum_up = copy(hc.at[0], hr.at[4], to_first(1))
+    via_down.wait_recv()
+    hc[1] = (hs[chunk[3], high].astype(F32) + hr[1].astype(F32)).astype(BF)
+    sum_down = copy(hc.at[1], hr.at[5], to_first(3))
+    grad_tpl(2)
+    grad_tpl(3)
+    stores = [
+        pltpu.make_async_copy(gt_out.at[pl.ds(128 * n, 128)], dst, store_sem.at[n])
+        for n, dst in enumerate((gt_low, gt_high))
+    ]
+    for store in stores:
+        store.start()
+    for part, direct, summed, a, b in ((low, own_down, sum_up, 3, 4), (high, own_up, sum_down, 2, 5)):
+        direct.wait_recv()
+        summed.wait_recv()
+        own = hs[first, part].astype(F32) + hr[a].astype(F32) + hr[b].astype(F32)
+        h2[part] = own.astype(BF)
     got = [copy(h2.at[(second + d) % 4], h2r.at[d - 1], to_second(d)) for d in (2, 1, 3)]
     for cp in got:
         cp.wait_recv()
@@ -359,7 +388,7 @@
     rs[...] = own.astype(BF)
 
     def block_copy(j):
-        ahead = (4 * k + j - c + 8) % 8
+        ahead = (4 * k + j + 12 - c) % 8
         near = z + ahead - 8 * (ahead // 5)
         slot = (ahead + 6) % 7
         return ahead, pltpu.make_async_remote_copy(
@@ -379,7 +408,12 @@
             src_ref=hp, dst_ref=hy.at[y % 2], send_sem=y_send.at[n], recv_sem=y_recv.at[y % 2],
             device_id=device(x, core, py, zh, c), device_id_type=MESH)
 
-    @pl.when(k == col_core)
+    def four_copy(n):
+        return pltpu.make_async_remote_copy(
+            src_ref=h_send, dst_ref=h_recv.at[n], send_sem=w_send.at[4 + n], recv_sem=w_recv_sem.at[7 + n],
+            device_id=to_z(z + 4 - 8 * n, k), device_id_type=MESH)
+
+    @pl.when(k != col_core)
     def _():
         own = rs[:, pl.ds(pl.multiple_of(128 * (c % 4), 128), 256)].astype(F32)
         for n in range(7):
@@ -388,12 +422,16 @@
                 device_id=sibling, device_id_type=MESH).wait_recv()
             own = own + w_recv[n].astype(F32)
         h_send[...] = own.astype(BF)
-        cp = pltpu.make_async_remote_copy(
-            src_ref=h_send, dst_ref=h_recv, send_sem=w_send.at[4], recv_sem=w_recv_sem.at[7],
-            device_id=across, device_id_type=MESH)
-        cp.start()
-        cp.wait()
-        whole = h_send[...].astype(F32) + h_recv[...].astype(F32)
+        for n in range(2):
+            four_copy(n).start()
+        for n in range(2):
+            four_copy(n).wait_send()
+
+    @pl.when(k == col_core)
+    def _():
+        for n in range(2):
+            four_copy(n).wait_recv()
+        whole = h_recv[0].astype(F32) + h_recv[1].astype(F32)
         hp[...] = pltpu.roll(whole, (256 - 32 * (c % 4)) % 256, 1).astype(BF)
         for d in (2, 1, 3):
             final_copy(d, row_core, (y + d) % 4).start()
@@ -429,6 +467,8 @@
         @pl.when(k != row_core)
         def _():
             final_copy(0, row_core, y).wait_send()
+    for store in stores:
+        store.wait()
     copy.finish()
 
 
@@ -437,6 +477,7 @@
     vm = pl.BlockSpec(memory_space=pltpu.VMEM)
     hbm = pl.BlockSpec(memory_space=pl.ANY)
     scratch = [
+        ((256, 1280), BF),
         ((256, 1280), BF), ((256, 1280), BF), ((160, 160), BF),
         ((80, 256), F32), ((80, 256), BF), ((4, 80, 256), BF), ((2, 4, 4, 80, 640), BF),
         ((2, 4, 4, 80, 256), BF), ((256, 1280), F32), ((256, 1), F32),
@@ -446,21 +487,22 @@
         ((256, 512), BF), ((2, 4, 4, 16, 640), BF), ((2, 3, 4, 16, 640), BF), ((2, 4, 16, 640), BF),
         ((2, 3, 16, 640), BF), ((16, 1280), BF), ((2, 16, 1280), BF),
         ((4, 16, 1280), BF), ((256, 1280), BF), ((256, 640), BF),
-        ((4, 4, 80, 640), BF), ((3, 4, 80, 640), BF), ((4, 80, 640), BF), ((3, 80, 640), BF),
-        ((80, 640), BF), ((7, 80, 256), BF), ((80, 256), BF), ((80, 256), BF), ((80, 256), BF),
+        ((4, 4, 80, 640), BF), ((6, 2, 80, 640), BF), ((2, 2, 80, 640), BF), ((4, 80, 640), BF), ((3, 80, 640), BF),
+        ((80, 640), BF), ((7, 80, 256), BF), ((80, 256), BF), ((2, 80, 256), BF), ((80, 256), BF),
         ((2, 80, 256), BF),
     ]
-    sems = (4, N_COPIES, N_COPIES, 8, 4, 5, 8, 4, 2)
-    gt, gp = pl.pallas_call(
+    sems = (4, 2, N_COPIES, N_COPIES, 9, 5, 6, 9, 4, 2)
+    gt_low, gt_high, gp = pl.pallas_call(
         kernel,
-        out_shape=(jax.ShapeDtypeStruct((256, 1280), BF), jax.ShapeDtypeStruct((160, 160), F32)),
+        out_shape=(jax.ShapeDtypeStruct((128, 1280), BF),) * 2 + (jax.ShapeDtypeStruct((160, 160), F32),),
         in_specs=[hbm] * 4,
-        out_specs=(vm, vm),
+        out_specs=(hbm, hbm, vm),
         scratch_shapes=[pltpu.VMEM(s, d) for s, d in scratch]
         + [pltpu.SemaphoreType.DMA((n,)) for n in sems],
         compiler_params=pltpu.CompilerParams(
             collective_id=0, has_side_effects=True, vmem_limit_bytes=60 << 20),
     )(images, labels.reshape(1, 256), flat, projection)
+    gt = jnp.concatenate([gt_low, gt_high], axis=0)
     return gt.reshape(templates.shape), gp
 
 

time: 128 us -> 126 us (0.984); the launches traced: 128 us -> 125 us
  Pallas kernels: 125 us -> 121 us
  local copies, waits for them, and re-layouts: 2.67 us -> 0.67 us
  other arithmetic: 0 us -> 1.99 us
    pallas_call x1, Pallas kernels: 125 us -> 121 us  [body(): pl.pallas_call(kernel, out_shape=(jax.ShapeDtypeStruct((128, 1280), BF),)...]
    unnamed x4 -> x3, local copies, waits for them, and re-layouts: 2.67 us -> 0.67 us
    concatenate x0 -> x1, other arithmetic: none -> 1.99 us  [body(): gt = jnp.concatenate([gt_low, gt_high], axis=0)]
where the time goes in v4:
time: 126 us; the launch traced here: 125 us
  Pallas kernels  121 us (96%)
  other arithmetic  1.99 us (2%)
    pallas_call x1, Pallas kernels, body(): pl.pallas_call(kernel, out_shape=(jax.ShapeDtypeStruct((128, 1280), BF),)...  121 us

profile of v4, /device:TPU:1, one launch (start us, length us, event | category | flops | bytes accessed | tf_op | source)
XLA Modules:
  0.0 124.8 jit_solution(6956445223529061353)
XLA Ops:
  0.6 121.5 %shard_map.59 = (bf16[128,1280]{1,0:T(8,128)(2,1)}, bf16[128,1280]{1,0:T(8,128)(2,1)}, f32[160,160]{1,0:T(8,128)}) custom-call(bf16[256,1280]{1,0:T(8,128)(2,1)} %images_in.1, s32[1,256]{1,0:T(1,128)} %bitcast.5, bf16[256,1280]{1,0:T(8,128)(2,1)} %bitcast.3, bf16[160,160]{1,0:T(8,128)(2,1)} %proj_in.1), custom_call_target="tpu_custom_call" | custom-call | tf_op jit(solution)/shard_map/pallas_call | solution.py:495
  122.1 0.0 copy-start
  122.1 2.0 %pad_maximum_fusion = bf16[256,1280]{1,0:T(8,128)(2,1)} fusion(bf16[128,1280]{1,0:T(8,128)(2,1)} %get-tuple-element.6, bf16[128,1280]{1,0:T(8,128)(2,1)} %get-tuple-element.5), kind=kLoop, calls=%fused_computation | loop fusion | flops 1310720 | bytes 1310720 | tf_op jit(solution)/shard_map/concatenate | solution.py:505
  124.1 0.0 copy-done
  124.1 0.7 copy.7
Async XLA Ops:
  122.1 2.0 %copy-start = (f32[160,160]{1,0:T(8,128)S(1)}, f32[160,160]{1,0:T(8,128)}, u32[]{:S(2)}) copy-start(f32[160,160]{1,0:T(8,128)} %get-tuple-element.11) | copy-start | bytes 307204

commit v5 on v4

--- a/solution.py
+++ b/solution.py
@@ -43,7 +43,7 @@
             cp.wait_send()
 
 
-N_COPIES = 190
+N_COPIES = 200
 
 
 def kernel(images_in, labels_in, tpl_in, proj_in, gt_low, gt_high, gp_out,
@@ -127,15 +127,6 @@
         def _():
             zb[c % 4] = pw[...]
 
-    for load in loads[1:]:
-        load.wait()
-    tt[k] = tpl[...].T.reshape(4, 4, 80, 256)
-    img_f = images[...].astype(F32)
-    img[k] = (img_f * inv_norm(img_f)).astype(BF)
-    to_img = copy(img.at[k], img.at[k], sibling)
-    to_lab = copy(lab.at[k], lab.at[k], sibling)
-    to_tx = copy(tt.at[k], tt.at[k], sibling)
-
     for j in range(4):
         block = 4 * k + j
 
@@ -182,6 +173,15 @@
         up[d1] = send(d1, 0, to_second(1))
         down[d1] = send(d1, 0, to_second(3))
         shared.append(send(d1, 0, sibling))
+    for load in loads[1:]:
+        load.wait()
+    tt[k] = tpl[...].T.reshape(4, 4, 80, 256)
+    img_f = images[...].astype(F32)
+    img[k] = (img_f * inv_norm(img_f)).astype(BF)
+    to_img = copy(img.at[k], img.at[k], sibling)
+    to_lab = copy(lab.at[k], lab.at[k], sibling)
+    to_tx = copy(tt.at[k], tt.at[k], sibling)
+
     far = {}
     for d1 in (0, 3, 1, 2):
         up[d1].wait_recv()
@@ -333,6 +333,28 @@
         return jnp.concatenate([tt[core, px, py] for px, py in [place(j, m) for m in range(4)]], axis=0)
 
     low, high = pl.ds(0, 2), pl.ds(2, 2)
+    parts = (pl.ds(0, 48), pl.ds(48, 32))
+    via_up, via_down, own_up, own_down, sum_up, sum_down = {}, {}, {}, {}, {}, {}
+
+    def send_via(p):
+        r = parts[p]
+        via_up[p] = copy(hs.at[chunk[2], low, r], hr.at[0, :, r], to_first(1))
+        via_down[p] = copy(hs.at[chunk[2], high, r], hr.at[1, :, r], to_first(3))
+
+    def send_own(p):
+        r = parts[p]
+        own_up[p] = copy(hs.at[chunk[1], high, r], hr.at[2, :, r], to_first(1))
+        own_down[p] = copy(hs.at[chunk[3], low, r], hr.at[3, :, r], to_first(3))
+
+    def send_sum(p):
+        r = parts[p]
+        via_up[p].wait_recv()
+        hc[0, :, r] = (hs[chunk[1], low, r].astype(F32) + hr[0, :, r].astype(F32)).astype(BF)
+        sum_up[p] = copy(hc.at[0, :, r], hr.at[4, :, r], to_first(1))
+        via_down[p].wait_recv()
+        hc[1, :, r] = (hs[chunk[3], high, r].astype(F32) + hr[1, :, r].astype(F32)).astype(BF)
+        sum_down[p] = copy(hc.at[1, :, r], hr.at[5, :, r], to_first(3))
+
     g_own = gz[:, half(k)]
     chunk = {d: (first + d) % 4 for d in range(4)}
     for d in (2, 1, 3, 0):
@@ -343,12 +365,9 @@
         v = v + jnp.dot(rows_of(other, chunk[d]), g_other, preferred_element_type=F32)
         hs[chunk[d]] = v.astype(BF).reshape(4, 80, 640)
         if d == 2:
-            via_up = copy(hs.at[chunk[2], low], hr.at[0], to_first(1))
-            via_down = copy(hs.at[chunk[2], high], hr.at[1], to_first(3))
-        elif d == 1:
-            own_up = copy(hs.at[chunk[1], high], hr.at[2], to_first(1))
+            send_via(0)
         elif d == 3:
-            own_down = copy(hs.at[chunk[3], low], hr.at[3], to_first(3))
+            send_own(0)
 
     def grad_tpl(m):
         v = 0.0
@@ -359,14 +378,12 @@
         gt_out[:, m * 320:(m + 1) * 320] = v.astype(BF)
 
     grad_tpl(0)
+    send_sum(0)
+    send_via(1)
+    send_own(1)
     grad_tpl(1)
-    via_up.wait_recv()
-    hc[0] = (hs[chunk[1], low].astype(F32) + hr[0].astype(F32)).astype(BF)
-    sum_up = copy(hc.at[0], hr.at[4], to_first(1))
-    via_down.wait_recv()
-    hc[1] = (hs[chunk[3], high].astype(F32) + hr[1].astype(F32)).astype(BF)
-    sum_down = copy(hc.at[1], hr.at[5], to_first(3))
     grad_tpl(2)
+    send_sum(1)
     grad_tpl(3)
     stores = [
         pltpu.make_async_copy(gt_out.at[pl.ds(128 * n, 128)], dst, store_sem.at[n])
@@ -374,99 +391,112 @@
     ]
     for store in stores:
         store.start()
-    for part, direct, summed, a, b in ((low, own_down, sum_up, 3, 4), (high, own_up, sum_down, 2, 5)):
-        direct.wait_recv()
-        summed.wait_recv()
-        own = hs[first, part].astype(F32) + hr[a].astype(F32) + hr[b].astype(F32)
-        h2[part] = own.astype(BF)
-    got = [copy(h2.at[(second + d) % 4], h2r.at[d - 1], to_second(d)) for d in (2, 1, 3)]
-    for cp in got:
-        cp.wait_recv()
-    own = h2[second].astype(F32)
-    for d in range(3):
-        own = own + h2r[d].astype(F32)
-    rs[...] = own.astype(BF)
-
-    def block_copy(j):
+    step = []
+    for p, r in enumerate(parts):
+        for m, direct, summed, a, b in (
+                (low, own_down, sum_up, 3, 4), (high, own_up, sum_down, 2, 5)):
+            direct[p].wait_recv()
+            summed[p].wait_recv()
+            own = hs[first, m, r].astype(F32) + hr[a, :, r].astype(F32) + hr[b, :, r].astype(F32)
+            h2[m, r] = own.astype(BF)
+        step.append([
+            copy(h2.at[(second + d) % 4, r], h2r.at[d - 1, r], to_second(d)) for d in (2, 1, 3)])
+
+    def block_copy(j, p):
         ahead = (4 * k + j + 12 - c) % 8
-        near = z + ahead - 8 * (ahead // 5)
+        near = z + ahead - 8 * ((ahead + p) // 5)
         slot = (ahead + 6) % 7
         return ahead, pltpu.make_async_remote_copy(
-            src_ref=rs.at[:, pl.ds(128 * j, 256)], dst_ref=w_recv.at[slot],
-            send_sem=w_send.at[j], recv_sem=w_recv_sem.at[slot],
+            src_ref=rs.at[parts[p], pl.ds(128 * j, 256)], dst_ref=w_recv.at[slot, parts[p]],
+            send_sem=w_send.at[2 * j + p], recv_sem=w_recv_sem.at[2 * slot + p],
             device_id=to_z(near, k), device_id_type=MESH)
 
-    for j in range(4):
-        ahead_j, cp = block_copy(j)
-
-        @pl.when(ahead_j != 0)
-        def _():
-            cp.start()
-
-    def final_copy(n, core, py):
+    for p, r in enumerate(parts):
+        for cp in step[p]:
+            cp.wait_recv()
+        own = h2[second, r].astype(F32)
+        for d in range(3):
+            own = own + h2r[d, r].astype(F32)
+        rs[r] = own.astype(BF)
+        for j in range(4):
+            ahead_j, cp = block_copy(j, p)
+
+            @pl.when(ahead_j != 0)
+            def _():
+                cp.start()
+
+    def four_copy(n, p):
         return pltpu.make_async_remote_copy(
-            src_ref=hp, dst_ref=hy.at[y % 2], send_sem=y_send.at[n], recv_sem=y_recv.at[y % 2],
+            src_ref=h_send.at[parts[p]], dst_ref=h_recv.at[n, parts[p]],
+            send_sem=w_send.at[8 + 2 * n + p], recv_sem=w_recv_sem.at[14 + 2 * n + p],
+            device_id=to_z(z + 4 - 8 * n, k), device_id_type=MESH)
+
+    def final_copy(n, p, core, py):
+        return pltpu.make_async_remote_copy(
+            src_ref=hp.at[parts[p]], dst_ref=hy.at[y % 2, parts[p]],
+            send_sem=y_send.at[2 * n + p], recv_sem=y_recv.at[2 * (y % 2) + p],
             device_id=device(x, core, py, zh, c), device_id_type=MESH)
-
-    def four_copy(n):
-        return pltpu.make_async_remote_copy(
-            src_ref=h_send, dst_ref=h_recv.at[n], send_sem=w_send.at[4 + n], recv_sem=w_recv_sem.at[7 + n],
-            device_id=to_z(z + 4 - 8 * n, k), device_id_type=MESH)
 
     @pl.when(k != col_core)
     def _():
-        own = rs[:, pl.ds(pl.multiple_of(128 * (c % 4), 128), 256)].astype(F32)
-        for n in range(7):
-            pltpu.make_async_remote_copy(
-                src_ref=h_send, dst_ref=w_recv.at[n], send_sem=w_send.at[0], recv_sem=w_recv_sem.at[n],
-                device_id=sibling, device_id_type=MESH).wait_recv()
-            own = own + w_recv[n].astype(F32)
-        h_send[...] = own.astype(BF)
-        for n in range(2):
-            four_copy(n).start()
-        for n in range(2):
-            four_copy(n).wait_send()
+        for p, r in enumerate(parts):
+            own = rs[r, pl.ds(pl.multiple_of(128 * (c % 4), 128), 256)].astype(F32)
+            for n in range(7):
+                pltpu.make_async_remote_copy(
+                    src_ref=h_send.at[r], dst_ref=w_recv.at[n, r], send_sem=w_send.at[0],
+                    recv_sem=w_recv_sem.at[2 * n + p], device_id=sibling, device_id_type=MESH).wait_recv()
+                own = own + w_recv[n, r].astype(F32)
+            h_send[r] = own.astype(BF)
+            for n in range(2):
+                four_copy(n, p).start()
+        for p in range(2):
+            for n in range(2):
+                four_copy(n, p).wait_send()
 
     @pl.when(k == col_core)
     def _():
-        for n in range(2):
-            four_copy(n).wait_recv()
-        whole = h_recv[0].astype(F32) + h_recv[1].astype(F32)
-        hp[...] = pltpu.roll(whole, (256 - 32 * (c % 4)) % 256, 1).astype(BF)
-        for d in (2, 1, 3):
-            final_copy(d, row_core, (y + d) % 4).start()
-
-        @pl.when(k != row_core)
-        def _():
-            final_copy(0, row_core, y).start()
-
-        @pl.when(k == row_core)
-        def _():
-            hy[y % 2] = hp[...]
+        for p, r in enumerate(parts):
+            for n in range(2):
+                four_copy(n, p).wait_recv()
+            whole = h_recv[0, r].astype(F32) + h_recv[1, r].astype(F32)
+            hp[r] = pltpu.roll(whole, (256 - 32 * (c % 4)) % 256, 1).astype(BF)
+            for d in (2, 1, 3):
+                final_copy(d, p, row_core, (y + d) % 4).start()
+
+            @pl.when(k != row_core)
+            def _():
+                final_copy(0, p, row_core, y).start()
+
+            @pl.when(k == row_core)
+            def _():
+                hy[y % 2, r] = hp[r]
 
     for n in range(2):
         @pl.when(jnp.logical_or(2 * k + n != y, k != col_core))
         def _():
-            pltpu.make_async_remote_copy(
-                src_ref=hp, dst_ref=hy.at[n], send_sem=y_send.at[0], recv_sem=y_recv.at[n],
-                device_id=sibling, device_id_type=MESH).wait_recv()
+            for p, r in enumerate(parts):
+                pltpu.make_async_remote_copy(
+                    src_ref=hp.at[r], dst_ref=hy.at[n, r], send_sem=y_send.at[0],
+                    recv_sem=y_recv.at[2 * n + p], device_id=sibling, device_id_type=MESH).wait_recv()
         gp_out[80 * n:80 * n + 80] = hy[n, :, 0:160].astype(F32)
 
-    for j in range(4):
-        ahead_j, cp = block_copy(j)
-
-        @pl.when(ahead_j != 0)
-        def _():
-            cp.wait_send()
+    for p in range(2):
+        for j in range(4):
+            ahead_j, cp = block_copy(j, p)
+
+            @pl.when(ahead_j != 0)
+            def _():
+                cp.wait_send()
 
     @pl.when(k == col_core)
     def _():
-        for d in (2, 1, 3):
-            final_copy(d, row_core, (y + d) % 4).wait_send()
-
-        @pl.when(k != row_core)
-        def _():
-            final_copy(0, row_core, y).wait_send()
+        for p in range(2):
+            for d in (2, 1, 3):
+                final_copy(d, p, row_core, (y + d) % 4).wait_send()
+
+            @pl.when(k != row_core)
+            def _():
+                final_copy(0, p, row_core, y).wait_send()
     for store in stores:
         store.wait()
     copy.finish()
@@ -491,7 +521,7 @@
         ((80, 640), BF), ((7, 80, 256), BF), ((80, 256), BF), ((2, 80, 256), BF), ((80, 256), BF),
         ((2, 80, 256), BF),
     ]
-    sems = (4, 2, N_COPIES, N_COPIES, 9, 5, 6, 9, 4, 2)
+    sems = (4, 2, N_COPIES, N_COPIES, 9, 5, 12, 18, 8, 4)
     gt_low, gt_high, gp = pl.pallas_call(
         kernel,
         out_shape=(jax.ShapeDtypeStruct((128, 1280), BF),) * 2 + (jax.ShapeDtypeStruct((160, 160), F32),),

time: 126 us -> 126 us (level); the launches traced: 125 us -> 126 us
  Pallas kernels: 121 us -> 123 us
    pallas_call x1, Pallas kernels: 121 us -> 123 us  [body(): pl.pallas_call(kernel, out_shape=(jax.ShapeDtypeStruct((128, 1280), BF),)...]
where the time goes in v5:
time: 126 us
  Pallas kernels  123 us (98%)
  other arithmetic  1.99 us (2%)
    pallas_call x1, Pallas kernels, body(): pl.pallas_call(kernel, out_shape=(jax.ShapeDtypeStruct((128, 1280), BF),)...  123 us

profile of v5, /device:TPU:1, one launch (start us, length us, event | category | flops | bytes accessed | tf_op | source)
XLA Modules:
  0.0 126.2 jit_solution(8888654367883742203)
XLA Ops:
  0.6 122.9 %shard_map.59 = (bf16[128,1280]{1,0:T(8,128)(2,1)}, bf16[128,1280]{1,0:T(8,128)(2,1)}, f32[160,160]{1,0:T(8,128)}) custom-call(bf16[256,1280]{1,0:T(8,128)(2,1)} %images_in.1, s32[1,256]{1,0:T(1,128)} %bitcast.5, bf16[256,1280]{1,0:T(8,128)(2,1)} %bitcast.3, bf16[160,160]{1,0:T(8,128)(2,1)} %proj_in.1), custom_call_target="tpu_custom_call" | custom-call | tf_op jit(solution)/shard_map/pallas_call | solution.py:525
  123.6 0.0 copy-start
  123.6 2.0 %pad_maximum_fusion = bf16[256,1280]{1,0:T(8,128)(2,1)} fusion(bf16[128,1280]{1,0:T(8,128)(2,1)} %get-tuple-element.6, bf16[128,1280]{1,0:T(8,128)(2,1)} %get-tuple-element.5), kind=kLoop, calls=%fused_computation | loop fusion | flops 1310720 | bytes 1310720 | tf_op jit(solution)/shard_map/concatenate | solution.py:535
  125.6 0.0 copy-done
  125.6 0.7 copy.7
Async XLA Ops:
  123.6 2.0 %copy-start = (f32[160,160]{1,0:T(8,128)S(1)}, f32[160,160]{1,0:T(8,128)}, u32[]{:S(2)}) copy-start(f32[160,160]{1,0:T(8,128)} %get-tuple-element.11) | copy-start | bytes 307204

commit v6 on v5

--- a/solution.py
+++ b/solution.py
@@ -82,6 +82,14 @@
     first, second = place(x, y)
     sibling = device(x, other, y, zh, c)
 
+    loads = [
+        pltpu.make_async_copy(src, dst, load_sem.at[n])
+        for n, (src, dst) in enumerate(
+            ((proj_in, proj), (tpl_in, tpl), (images_in, images), (labels_in, lab.at[k])))
+    ]
+    for load in loads:
+        load.start()
+
     barrier = pltpu.get_barrier_semaphore()
     peers = [to_plane(dx, dy) for dx, dy in PLANE]
     peers += [to_z(z + d, k) for d in RING]
@@ -89,14 +97,6 @@
     peers += [device(x, other, (y + d) % 4, zh, c) for d in range(4)]
     for peer in peers:
         pl.semaphore_signal(barrier, inc=1, device_id=peer, device_id_type=MESH)
-
-    loads = [
-        pltpu.make_async_copy(src, dst, load_sem.at[n])
-        for n, (src, dst) in enumerate(
-            ((proj_in, proj), (tpl_in, tpl), (images_in, images), (labels_in, lab.at[k])))
-    ]
-    for load in loads:
-        load.start()
 
     copy = Copies(send_sem, recv_sem)
 
@@ -164,7 +164,7 @@
     def send(d1, d2, to):
         return copy(piece(d1, d2), piece(d1, d2), to)
 
-    shared = []
+    shared, far = [], {}
     ahead = {d: send(0, 0, to_first(d)) for d in (1, 3, 2)}
     up, down = {}, {}
     for d1 in (0, 3, 1, 2):
@@ -172,6 +172,8 @@
             ahead[(4 - d1) % 4].wait_recv()
         up[d1] = send(d1, 0, to_second(1))
         down[d1] = send(d1, 0, to_second(3))
+        if d1 == 2:
+            far[d1] = send(d1, 0, to_second(2))
         shared.append(send(d1, 0, sibling))
     for load in loads[1:]:
         load.wait()
@@ -182,13 +184,12 @@
     to_lab = copy(lab.at[k], lab.at[k], sibling)
     to_tx = copy(tt.at[k], tt.at[k], sibling)
 
-    far = {}
     for d1 in (0, 3, 1, 2):
         up[d1].wait_recv()
         if d1 in (0, 3):
             far[d1] = send(d1, 3, to_second(1))
         down[d1].wait_recv()
-        if d1 in (1, 2):
+        if d1 == 1:
             far[d1] = send(d1, 1, to_second(3))
         shared.append(send(d1, 3, sibling))
         shared.append(send(d1, 1, sibling))
@@ -321,13 +322,14 @@
     for cp in [copy(gs.at[y], gs.at[y], to_plane(0, d)) for d in (2, 1, 3)]:
         cp.wait_recv()
     per_u = gs[...].reshape(64, 1280).astype(F32)
+    to_gx = []
     for n in range(4):
         rows_n = slice(n * 64, (n + 1) * 64)
         u = zbuf[rows_n]
         inner = jnp.sum(u * per_u, axis=1, keepdims=True)
         gz[rows_n] = ((per_u - u * inner) * rzbuf[rows_n]).astype(BF)
-
-    to_gx = copy(gz.at[:, half(other)], gx, sibling)
+        r = pl.ds(64 * n, 64)
+        to_gx.append(copy(gz.at[r, half(other)], gx.at[r], sibling))
 
     def rows_of(core, j):
         return jnp.concatenate([tt[core, px, py] for px, py in [place(j, m) for m in range(4)]], axis=0)
@@ -360,7 +362,8 @@
     for d in (2, 1, 3, 0):
         v = jnp.dot(rows_of(k, chunk[d]), g_own, preferred_element_type=F32)
         if d == 2:
-            to_gx.wait_recv()
+            for cp in to_gx:
+                cp.wait_recv()
             g_other = gx[...]
         v = v + jnp.dot(rows_of(other, chunk[d]), g_other, preferred_element_type=F32)
         hs[chunk[d]] = v.astype(BF).reshape(4, 80, 640)

time: 126 us -> 125 us (level)
  no operation moved by 1% of the time
where the time goes in v6:
time: 125 us
  Pallas kernels  122 us (98%)
  other arithmetic  1.99 us (2%)
    pallas_call x1, Pallas kernels, body(): pl.pallas_call(kernel, out_shape=(jax.ShapeDtypeStruct((128, 1280), BF),)...  122 us

profile of v6, /device:TPU:1, one launch (start us, length us, event | category | flops | bytes accessed | tf_op | source)
XLA Modules:
  0.0 125.0 jit_solution(762973226416188542)
XLA Ops:
  0.6 121.7 %shard_map.59 = (bf16[128,1280]{1,0:T(8,128)(2,1)}, bf16[128,1280]{1,0:T(8,128)(2,1)}, f32[160,160]{1,0:T(8,128)}) custom-call(bf16[256,1280]{1,0:T(8,128)(2,1)} %images_in.1, s32[1,256]{1,0:T(1,128)} %bitcast.5, bf16[256,1280]{1,0:T(8,128)(2,1)} %bitcast.3, bf16[160,160]{1,0:T(8,128)(2,1)} %proj_in.1), custom_call_target="tpu_custom_call" | custom-call | tf_op jit(solution)/shard_map/pallas_call | solution.py:528
  122.4 0.0 copy-start
  122.4 2.0 %pad_maximum_fusion = bf16[256,1280]{1,0:T(8,128)(2,1)} fusion(bf16[128,1280]{1,0:T(8,128)(2,1)} %get-tuple-element.6, bf16[128,1280]{1,0:T(8,128)(2,1)} %get-tuple-element.5), kind=kLoop, calls=%fused_computation | loop fusion | flops 1310720 | bytes 1310720 | tf_op jit(solution)/shard_map/concatenate | solution.py:538
  124.4 0.0 copy-done
  124.4 0.7 copy.7
Async XLA Ops:
  122.4 2.0 %copy-start = (f32[160,160]{1,0:T(8,128)S(1)}, f32[160,160]{1,0:T(8,128)}, u32[]{:S(2)}) copy-start(f32[160,160]{1,0:T(8,128)} %get-tuple-element.11) | copy-start | bytes 307204
